TPU v7x, 128 devices: a whole 4x4x4 slice. The times are simulated.
128 devices in a mesh: seq: 16 (over x, z), tp: 4 (over y_lo, core), img: 2 (over y_hi).
Axes of the slice: x: 4, y: 4 (y_hi: 2, y_lo: 2; y = y_hi * 2 + y_lo), z: 4, core: 2. Of those that a mesh axis runs over, the one named last changes fastest.
Arguments:
- patches: bfloat16 [16, 1024, 1280], P('seq'), may hold values from -6 to 6
- patch_counts: int32 [16], P('seq'), may hold values from 64 to 1024, as said below
- image_offsets: int32 [16], P('seq'), may hold values from 0 to 8191, as said below
- vision_gain: float32 [1280], replicated, may hold values from 0.1 to 1.9
- vision_shift: float32 [1280], replicated, may hold values from -3 to 3
- vision_qkv: bfloat16 [1280, 3840], P(None, ('tp', 'img'))
- vision_qkv_bias: bfloat16 [3840], P(('tp', 'img')), may hold values from -3 to 3
- vision_proj: bfloat16 [1280, 1280], P(('tp', 'img')), may hold values from -0.15625 to 0.15625
- vision_proj_bias: float32 [1280], replicated, may hold values from -3 to 3
- merge_gain: float32 [1280], replicated, may hold values from 0.1 to 1.9
- merge_shift: float32 [1280], replicated, may hold values from -3 to 3
- merge_weight: bfloat16 [5120, 8192], P(None, ('tp', 'img')), may hold values from -0.078125 to 0.078125
- merge_bias: bfloat16 [8192], P(('tp', 'img')), may hold values from -3 to 3
- text_embed: bfloat16 [8192, 8192], P(('seq', 'img'), 'tp'), may hold values from -6 to 6
- norm_gain: bfloat16 [8192], replicated, may hold values from 0.099609375 to 1.8984375
- qkv_weight: bfloat16 [8192, 5120], P(('seq', 'img'), 'tp')
- qkv_bias: bfloat16 [5120], P('tp'), may hold values from -3 to 3
Outputs:
- attention_out: bfloat16 [8192, 4096], P(('seq', 'img'), 'tp')
Inputs may be any that keep to these rules, and one draw needn't show every extreme that they name: `patch_counts`: each a multiple of 4; one image in every draw has all 1024 slots filled. The merged tokens of image s take the positions image_offsets[s] to image_offsets[s] + patch_counts[s] / 4 - 1, all within s * 512 to (s + 1) * 512 - 1.
All inputs are finite; a program needn't handle non-finite values.
Results may differ from a plain program's by a relative error of at most 0.0065.
Values may be sent and summed in bfloat16 or wider, within the bound.
A program may use at most 128 MiB of HBM per device.

v0:
```python
import jax
import jax.numpy as jnp
from jax import lax
from jax.sharding import PartitionSpec as P

HEAD = 128
VW = 1280
PATCH_CAP = 1024
GROUP = 8
VHEAD = 80


EPSILON = 1e-06
THETA = 1000000.0
MASKED = -1e30


def layer_norm(source, scaling, shifting):
    average = jnp.mean(source, axis=-1, keepdims=True)
    centred = source - average
    spread = jnp.mean(centred * centred, axis=-1, keepdims=True)
    return centred * lax.rsqrt(spread + EPSILON) * scaling + shifting


def rotary(inputs, positions, head_width):
    halfway = head_width // 2
    frequency = jnp.power(
        jnp.float32(THETA), -(jnp.arange(halfway, dtype=jnp.float32) * 2.0) / head_width
    )
    angles = positions.astype(jnp.float32)[:, None] * frequency[None, :]
    angles = angles.reshape((angles.shape[0],) + (1,) * (inputs.ndim - 2) + (halfway,))
    cosine = jnp.cos(angles)
    sine_value = jnp.sin(angles)
    leading = inputs[..., :halfway]
    trailing = inputs[..., halfway:]
    return jnp.concatenate(
        [leading * cosine - trailing * sine_value, trailing * cosine + leading * sine_value],
        axis=-1,
    )


def keep_state(state_in):
    return state_in


def on_device(
    patches,
    patch_counts,
    image_offsets,
    vision_gain,
    vision_shift,
    vision_qkv,
    vision_qkv_bias,
    vision_proj,
    vision_proj_bias,
    merge_gain,
    merge_shift,
    merge_weight,
    merge_bias,
    text_embed,
    norm_gain,
    qkv_weight,
    qkv_bias,
):
    count = patch_counts[0]
    offset = image_offsets[0]
    source = patches[0].astype(jnp.float32)
    normed_patches = layer_norm(source, vision_gain, vision_shift).astype(jnp.bfloat16)
    local_heads = vision_qkv.shape[1] // (3 * VHEAD)
    mixed = jnp.dot(
        normed_patches, vision_qkv, preferred_element_type=jnp.float32
    ) + vision_qkv_bias.astype(jnp.float32)
    mixed = mixed.astype(jnp.bfloat16).reshape(PATCH_CAP, local_heads, 3, VHEAD)
    scores = jnp.einsum(
        "qhe,khe->hqk", mixed[:, :, 0], mixed[:, :, 1], preferred_element_type=jnp.float32
    )
    scores = scores * VHEAD ** (-0.5)
    valid = jnp.arange(PATCH_CAP, dtype=jnp.int32) < count
    scores = jnp.where(valid[None, None, :], scores, MASKED)
    top_score = jnp.max(scores, axis=-1, keepdims=True)
    raw = jnp.where(valid[None, None, :], jnp.exp(scores - top_score), 0.0)
    totals = jnp.sum(raw, axis=-1)
    context = jnp.einsum(
        "hqk,khe->qhe", raw.astype(jnp.bfloat16), mixed[:, :, 2], preferred_element_type=jnp.float32
    )
    context = (context / jnp.transpose(totals)[:, :, None]).astype(jnp.bfloat16)
    context = context.reshape(PATCH_CAP, local_heads * VHEAD)
    partial_proj = jnp.dot(context, vision_proj, preferred_element_type=jnp.float32)
    summed = lax.psum(partial_proj, ("tp", "img"))
    resid = summed + vision_proj_bias + source
    merge_rows = layer_norm(resid, merge_gain, merge_shift).astype(jnp.bfloat16)
    merge_in = merge_rows.reshape(PATCH_CAP // 4, 4 * VW)
    token_part = jnp.dot(
        merge_in, merge_weight, preferred_element_type=jnp.float32
    ) + merge_bias.astype(jnp.float32)
    token_cols = lax.all_gather(token_part.astype(jnp.bfloat16), "img", axis=1, tiled=True)
    tok_rows = text_embed.shape[0]
    my_start = lax.axis_index(("seq", "img")) * tok_rows
    padded = jnp.pad(token_cols, ((tok_rows, tok_rows), (0, 0)))
    where_at = jnp.clip(my_start - offset + tok_rows, 0, PATCH_CAP // 4 + tok_rows)
    placed = lax.dynamic_slice_in_dim(padded, where_at, tok_rows, 0)
    positions = my_start + jnp.arange(tok_rows, dtype=jnp.int32)
    inside = (positions >= offset) & (positions < offset + count // 4)
    hidden = jnp.where(inside[:, None], placed, text_embed)
    full_rows = lax.all_gather(hidden, "tp", axis=1, tiled=True)
    wide = full_rows.astype(jnp.float32)
    normed = (
        wide
        * lax.rsqrt(jnp.mean(wide * wide, axis=-1, keepdims=True) + EPSILON)
        * norm_gain.astype(jnp.float32)
    )
    normed = normed.astype(jnp.bfloat16)
    columns_out = qkv_weight.shape[1]
    projected = jnp.dot(
        normed,
        lax.all_gather(qkv_weight, ("seq", "img"), axis=0, tiled=True),
        preferred_element_type=jnp.float32,
    )
    projected = projected + qkv_bias.astype(jnp.float32)
    local_groups = columns_out // ((GROUP + 2) * HEAD)
    projected = projected.reshape(tok_rows, local_groups, GROUP + 2, HEAD)
    queries = rotary(projected[:, :, :GROUP], positions, HEAD).astype(jnp.bfloat16)
    keys = rotary(projected[:, :, GROUP], positions, HEAD).astype(jnp.bfloat16)
    values = projected[:, :, GROUP + 1].astype(jnp.bfloat16)
    last_pos = my_start + tok_rows - 1
    initial = (
        jnp.full((local_groups, GROUP, tok_rows), MASKED, jnp.float32),
        jnp.zeros((local_groups, GROUP, tok_rows), jnp.float32),
        jnp.zeros((local_groups, GROUP, tok_rows, HEAD), jnp.float32),
    )
    start = jnp.int32(0)
    key_piece = lax.all_gather(keys, ("seq", "img"), axis=0, tiled=True)
    value_piece = lax.all_gather(values, ("seq", "img"), axis=0, tiled=True)
    length = key_piece.shape[0]
    key_width = max(
        (candidate for candidate in range(1, min(length, 512) + 1) if length % candidate == 0)
    )
    block_count = length // key_width
    key_blocks = key_piece.reshape(block_count, key_width, local_groups, HEAD)
    value_blocks = value_piece.reshape(block_count, key_width, local_groups, HEAD)

    def step_block(state, items):
        key_block, value_block, number = items
        first_key = start + number * key_width

        def compute(state_in):
            top_run, total_run, running = state_in
            block_scores = jnp.einsum(
                "qgae,kge->gaqk", queries, key_block, preferred_element_type=jnp.float32
            )
            block_scores = block_scores * HEAD ** (-0.5)
            key_pos = first_key + jnp.arange(key_width, dtype=jnp.int32)
            allowed = key_pos[None, :] <= positions[:, None]
            block_scores = jnp.where(allowed, block_scores, MASKED)
            new_top = jnp.maximum(top_run, jnp.max(block_scores, axis=-1))
            factor = jnp.exp(top_run - new_top)
            weights = jnp.where(allowed, jnp.exp(block_scores - new_top[..., None]), 0.0)
            total_new = total_run * factor + jnp.sum(weights, axis=-1)
            running_new = running * factor[..., None] + jnp.einsum(
                "gaqk,kge->gaqe",
                weights.astype(jnp.bfloat16),
                value_block,
                preferred_element_type=jnp.float32,
            )
            return (new_top, total_new, running_new)

        return (lax.cond(first_key <= last_pos, compute, keep_state, state), None)

    result, unused = lax.scan(
        step_block, initial, (key_blocks, value_blocks, jnp.arange(block_count, dtype=jnp.int32))
    )
    state = result
    top_final, total_final, running_final = state
    output = running_final / total_final[..., None]
    output = jnp.transpose(output, (2, 0, 1, 3)).reshape(tok_rows, local_groups * GROUP * HEAD)
    return output.astype(jnp.bfloat16)


def solution(mesh):
    placed = (
        P("seq", None, None),
        P("seq"),
        P("seq"),
        P(),
        P(),
        P(None, ("tp", "img")),
        P(("tp", "img")),
        P(("tp", "img"), None),
        P(),
        P(),
        P(),
        P(None, ("tp", "img")),
        P(("tp", "img")),
        P(("seq", "img"), "tp"),
        P(),
        P(("seq", "img"), "tp"),
        P("tp"),
    )
    return jax.shard_map(
        on_device, mesh=mesh, in_specs=placed, out_specs=P(("seq", "img"), "tp"), check_vma=False
    )
```

profile of v0, /device:TPU:102, one launch (start us, length us, event | category | flops | bytes accessed | tf_op | source)
XLA Modules:
  0.0 659.9 jit_solution(16548593072326590953)
XLA Ops:
  12.4 6.0 fusion.87
  21.5 3.3 fusion.88
  25.5 77.3 %all-reduce.3.cloned.1.call-done = f32[1024,1280]{1,0:T(8,128)} async-done(((f32[1024,1280]{1,0:T(8,128)}), f32[1024,1280]{1,0:T(8,128)}) %all-reduce.3.cloned.1.call-update) | async-done | bytes 5242896 | tf_op jit(solution)/shard_map/psum | solution.py:89
  102.8 4.2 fusion.60
  107.6 3.1 multiply_reduce_fusion
  113.4 5.2 reshape.352
  118.7 8.5 %fusion.61 = bf16[256,1024]{1,0:T(8,128)(2,1)} fusion(bf16[256,5120]{1,0:T(8,128)(2,1)} %reshape.352, bf16[5120,1024]{1,0:T(8,128)(2,1)} %param.32, f32[1024]{0:T(1024)S(1)} %convert_element_type.107), kind=kOutput, calls=%fused_computation.68 | convolution fusion | flops 2684878848 | bytes 13635584 | tf_op jit(solution)/shard_map/dot_general | solution.py:93
  127.9 24.9 %all-gather.7.cloned.1.call-done = bf16[256,2048]{1,0:T(8,128)(2,1)} async-done(((bf16[256,1024]{1,0:T(8,128)(2,1)}), bf16[256,2048]{1,0:T(8,128)(2,1)}) %all-gather.7.cloned.1.call-update) | async-done | bytes 1048592 | tf_op jit(solution)/shard_map/all_gather | solution.py:96
  156.6 44.7 %all-gather.9.cloned.1.call-done = bf16[256,8192]{1,0:T(8,128)(2,1)} async-done(((bf16[256,2048]{1,0:T(8,128)(2,1)}), bf16[256,8192]{1,0:T(8,128)(2,1)}) %all-gather.9.cloned.1.call-update) | async-done | bytes 4194320 | tf_op jit(solution)/shard_map/all_gather | solution.py:105
  204.4 180.3 %all-gather.11.cloned.1.call-done = bf16[8192,1280]{1,0:T(8,128)(2,1)} async-done(((bf16[256,1280]{1,0:T(8,128)(2,1)}), bf16[8192,1280]{1,0:T(8,128)(2,1)}) %all-gather.11.cloned.1.call-update) | async-done | bytes 20971536 | tf_op jit(solution)/shard_map/all_gather | solution.py:116
  384.7 14.4 %fusion.49 = f32[256,1280]{1,0:T(8,128)} fusion(bf16[8192,1280]{1,0:T(8,128)(2,1)} %all-gather.11.cloned.1.call-done, bf16[256,8192]{1,0:T(8,128)(2,1)} %all-gather.9.cloned.1.call-done, f32[8192]{0:T(1024)S(1)} %convert_element_type.110, f32[256]{0:T(256)S(1)} %add_rsqrt_fusion.2, f32[1280]{0:T(1024)S(1)} %convert_element_type.112), kind=kOutput, calls=%fused_computation.59 | convolution fusion | flops 5377425408 | bytes 26515456 | tf_op jit(solution)/shard_map/dot_general | solution.py:114
  403.5 64.9 %all-gather.13.cloned.1.call-done = bf16[8192,1,128]{0,2,1:T(8,128)(2,1)} async-done(((bf16[256,1,128]{0,2,1:T(8,128)(2,1)}), bf16[8192,1,128]{0,2,1:T(8,128)(2,1)}) %all-gather.13.cloned.1.call-update) | async-done | bytes 2097168 | tf_op jit(solution)/shard_map/all_gather | solution.py:132
  468.4 4.1 copy.39
  472.4 66.9 %all-gather.15.cloned.1.call-done = bf16[8192,1,1,128]{0,3,2,1:T(8,128)(2,1)} async-done(((bf16[256,1,1,128]{0,3,2,1:T(8,128)(2,1)}), bf16[8192,1,1,128]{0,3,2,1:T(8,128)(2,1)}) %all-gather.15.cloned.1.call-update) | async-done | bytes 2097168 | tf_op jit(solution)/shard_map/all_gather | solution.py:133
  539.4 4.1 copy.32
  543.5 107.9 %while.15 = (s32[]{:T(128)}, f32[1,8,256]{2,1,0:T(8,128)S(1)}, f32[1,8,256]{2,1,0:T(8,128)S(1)}, f32[1,8,256,128]{3,2,1,0:T(8,128)S(1)}, s32[16]{0:T(128)S(1)}, ...) while((s32[]{:T(128)}, f32[1,8,256]{2,1,0:T(8,128)S(1)}, ...), condition=%wide.region_13.14_spmd.clone, body=%wide.region_8.13_spmd.clone.sunk | while | flops 551164672 | bytes 16131371 | solution.py:169
  544.8 5.5 conditional.3
  551.6 5.5 conditional.3
  558.3 5.5 conditional.3
  565.0 5.5 conditional.3
  571.8 5.5 conditional.3
  578.5 5.5 conditional.3
  585.3 5.5 conditional.3
  592.0 5.5 conditional.3
  598.8 5.5 conditional.3
  605.5 5.5 conditional.3
  612.2 5.5 conditional.3
  619.0 5.5 conditional.3
  625.7 5.5 conditional.3
  632.5 5.5 conditional.3
  639.2 5.5 conditional.3
  645.9 5.5 conditional.3
  (256 shorter events, 120.6 us)
Async XLA Ops:
  6.5 4.2 copy-start
  6.5 4.1 copy-start.13
  6.5 4.2 copy-start.15
  6.5 4.2 copy-start.14
  6.5 96.3 %all-reduce.3.cloned.1.call-start = ((), (), s32[]{:S(2)}) async-start(), calls=%async_computation | async-start | bytes 10485760 | tf_op jit(solution)/shard_map/psum | solution.py:89
  6.6 3.2 copy-start.2
  18.4 3.1 copy-start.6
  24.8 0.7 copy-start.12
  24.8 78.0 %copy-start.7 = (f32[1280]{0:T(1024)S(1)}, f32[1280]{0:T(1024)}, u32[]{:S(2)}) copy-start(f32[1280]{0:T(1024)} %param.29) | copy-start | bytes 15364
  24.8 128.1 %all-gather.7.cloned.1.call-start = ((), (), s32[]{:S(2)}) async-start(), calls=%async_computation.1 | async-start | bytes 1572864 | tf_op jit(solution)/shard_map/all_gather | solution.py:96
  102.8 4.8 copy-start.4
  107.0 3.7 copy-start.3
  107.0 3.7 copy-start.9
  107.0 3.7 copy-start.10
  118.6 34.2 %copy-start.5 = (bf16[256,2048]{1,0:T(8,128)(2,1)S(1)}, bf16[256,2048]{1,0:T(8,128)(2,1)}, u32[]{:S(2)}) copy-start(bf16[256,2048]{1,0:T(8,128)(2,1)} %param.34) | copy-start | bytes 3145732
  127.2 29.4 %copy-start.8 = (bf16[8192]{0:T(1024)(128)(2,1)S(1)}, bf16[8192]{0:T(1024)(128)(2,1)}, u32[]{:S(2)}) copy-start(bf16[8192]{0:T(1024)(128)(2,1)} %param.35) | copy-start | bytes 49156
  127.2 29.4 %copy-start.11 = (bf16[1280]{0:T(1024)(128)(2,1)S(1)}, bf16[1280]{0:T(1024)(128)(2,1)}, u32[]{:S(2)}) copy-start(bf16[1280]{0:T(1024)(128)(2,1)} %param.37) | copy-start | bytes 7684
  127.2 74.1 %all-gather.9.cloned.1.call-start = ((), (), s32[]{:S(2)}) async-start(), calls=%async_computation.2 | async-start | bytes 5242880 | tf_op jit(solution)/shard_map/all_gather | solution.py:105
  155.9 228.8 %all-gather.11.cloned.1.call-start = ((), (), s32[]{:S(2)}) async-start(), calls=%async_computation.3 | async-start | bytes 21626880 | tf_op jit(solution)/shard_map/all_gather | solution.py:116
  156.5 311.9 %all-gather.13.cloned.1.call-start = ((), (), s32[]{:S(2)}) async-start(), calls=%async_computation.4 | async-start | bytes 2162688 | tf_op jit(solution)/shard_map/all_gather | solution.py:132
  401.8 137.6 %all-gather.15.cloned.1.call-start = ((), (), s32[]{:S(2)}) async-start(), calls=%async_computation.5 | async-start | bytes 2162688 | tf_op jit(solution)/shard_map/all_gather | solution.py:133
  651.4 1.6 copy-start.1
Sparse Core Ops, SparseCore 0:
  24.9 77.8 all-reduce.2
  127.3 25.5 all-gather.6
  156.0 45.1 all-gather.8
  204.2 180.4 all-gather.10
  401.9 66.4 all-gather.12
  471.0 68.3 all-gather.14
where the time goes:
time: 661 us; the launch traced here: 660 us
  waiting for transfers between devices  460 us (70%)
  matrix products  104 us (16%)
  other arithmetic  40.1 us (6%)
  local copies, waits for them, and re-layouts  27.8 us (4%)
  between operations  15.3 us (2%)
  loops' own time  12.2 us (2%)
    all_gather x1, waiting for transfers between devices, on_device(): lax.all_gather(qkv_weight, ('seq', 'img'), axis=0, tiled=True)  180 us
    psum x1, waiting for transfers between devices, on_device(): summed = lax.psum(partial_proj, ('tp', 'img'))  77.3 us
    all_gather x1, waiting for transfers between devices, on_device(): value_piece = lax.all_gather(values, ('seq', 'img'), axis=0, tiled=True)  66.9 us
    all_gather x1, waiting for transfers between devices, on_device(): key_piece = lax.all_gather(keys, ('seq', 'img'), axis=0, tiled=True)  64.9 us
    all_gather x1, waiting for transfers between devices, on_device(): full_rows = lax.all_gather(hidden, 'tp', axis=1, tiled=True)  44.7 us
    dot_general x16, matrix products, compute(): jnp.einsum('gaqk,kge->gaqe', weights.astype(jnp.bfloat16), value_block, p...  40.3 us
    dot_general x16, matrix products, compute(): jnp.einsum('qgae,kge->gaqk', queries, key_block, preferred_element_type=j...  26.9 us
    all_gather x1, waiting for transfers between devices, on_device(): lax.all_gather(token_part.astype(jnp.bfloat16), 'img', axis=1, tiled=True)  24.9 us
  transfers between devices with their start and end apart: 6, of which 6 were waited for; matrix products, arithmetic and copies ran while one was open for 1% of the time, Pallas kernels for 0%

commit v1 on v0

v1 whole, which is shorter than its diff:
```python
import functools

import jax
import jax.numpy as jnp
from jax import lax
from jax.experimental import pallas as pl
from jax.experimental.pallas import tpu as pltpu
from jax.sharding import PartitionSpec as P

HEAD = 128
VW = 1280
PATCH_CAP = 1024
GROUP = 8
VHEAD = 80
SECTION = 512
HALF = 256
OWN_HEADS = 4

EPSILON = 1e-06
THETA = 1000000.0
MASKED = -1e30
LOG2E = 1.4426950408889634
MESH = pl.DeviceIdType.MESH


def layer_norm(source, scaling, shifting):
    average = jnp.mean(source, axis=-1, keepdims=True)
    centred = source - average
    spread = jnp.mean(centred * centred, axis=-1, keepdims=True)
    return centred * lax.rsqrt(spread + EPSILON) * scaling + shifting


def rotary(inputs, positions, head_width):
    halfway = head_width // 2
    frequency = jnp.power(
        jnp.float32(THETA), -(jnp.arange(halfway, dtype=jnp.float32) * 2.0) / head_width
    )
    angles = positions.astype(jnp.float32)[:, None] * frequency[None, :]
    angles = angles.reshape((angles.shape[0],) + (1,) * (inputs.ndim - 2) + (halfway,))
    cosine = jnp.cos(angles)
    sine_value = jnp.sin(angles)
    leading = inputs[..., :halfway]
    trailing = inputs[..., halfway:]
    return jnp.concatenate(
        [leading * cosine - trailing * sine_value, trailing * cosine + leading * sine_value],
        axis=-1,
    )


def attend_kernel(x_ref, out_ref, buf, ext, other, top, acc, send, recv):
    seq = lax.axis_index("seq")
    img = lax.axis_index("img")
    x = seq // 4
    z = seq % 4
    partner = {"img": 1 - img}

    def along_x(d):
        return {"seq": ((x + d) % 4) * 4 + z}

    def along_z(d):
        return {"seq": x * 4 + (z + d) % 4}

    peers = [partner] + [along_x(d) for d in (1, 2, 3)] + [along_z(d) for d in (1, 2, 3)]
    barrier = pltpu.get_barrier_semaphore()
    for peer in peers:
        pl.semaphore_signal(barrier, inc=1, device_id=peer, device_id_type=MESH)
    pl.semaphore_wait(barrier, len(peers))

    def copy(src, dst, number, peer):
        return pltpu.make_async_remote_copy(
            src_ref=src,
            dst_ref=dst,
            send_sem=send.at[number],
            recv_sem=recv.at[number],
            device_id=peer,
            device_id_type=MESH,
        )

    buf[img, x, z] = x_ref[:, OWN_HEADS * HEAD :]
    own = buf.at[img, x, z]
    swap = copy(own, own, 0, partner)
    swap.start()
    swap.wait()
    first, second = pl.ds(0, HALF), pl.ds(HALF, HALF)
    part_a = buf.at[:, x, z, first]
    part_b = buf.at[:, x, z, second]
    one = [copy(part_a, part_a, d, along_x(d)) for d in (1, 2, 3)]
    two = [copy(part_b, part_b, 3 + d, along_z(d)) for d in (1, 2, 3)]
    for c in one + two:
        c.start()
    for c in one:
        c.wait()
    part_c = buf.at[:, :, z, first]
    three = [copy(part_c, part_c, 6 + d, along_z(d)) for d in (1, 2, 3)]
    for c in three:
        c.start()
    for c in two:
        c.wait()
    part_d = buf.at[:, x, :, second]
    four = [copy(part_d, part_d, 9 + d, along_x(d)) for d in (1, 2, 3)]
    for c in four:
        c.start()

    top[...] = jnp.full_like(top, MASKED)
    acc[...] = jnp.zeros_like(acc)
    ones = jnp.ones((SECTION, HEAD), jnp.bfloat16)

    def block(half, rows, head, keys, values, mask):
        query = x_ref[rows, head * HEAD : (head + 1) * HEAD]
        scores = lax.dot_general(
            query, keys, (((1,), (1,)), ((), ())), preferred_element_type=jnp.float32
        )
        scores = scores * (HEAD ** (-0.5) * LOG2E)
        if mask is not None:
            scores = jnp.where(mask, scores, MASKED)
        old = top[half, head]
        new = jnp.maximum(old, jnp.max(scores, axis=-1, keepdims=True))
        factor = jnp.exp2(old - new)
        weights = jnp.exp2(scores - new[:, :1]).astype(jnp.bfloat16)
        product = jnp.dot(weights, values, preferred_element_type=jnp.float32)
        top[half, head] = new
        acc[half, head] = acc[half, head] * jnp.concatenate([factor, factor], axis=1) + product

    def diagonal(half):
        rows = pl.ds(half * HALF, HALF)
        keys = buf[0, x, z]
        values = jnp.concatenate([buf[1, x, z], ones], axis=1)
        row = lax.broadcasted_iota(jnp.int32, (HALF, SECTION), 0) + half * HALF
        col = lax.broadcasted_iota(jnp.int32, (HALF, SECTION), 1)
        mask = col <= row
        for head in range(OWN_HEADS):
            block(half, rows, head, keys, values, mask)

    def earlier(half, number):
        rows = pl.ds(half * HALF, HALF)
        keys = buf[0, number // 4, number % 4]
        values = jnp.concatenate([buf[1, number // 4, number % 4], ones], axis=1)
        for head in range(OWN_HEADS):
            block(half, rows, head, keys, values, None)

    def finish(half):
        parts = []
        for head in range(OWN_HEADS):
            total = acc[half, head]
            parts.append((total[:, :HEAD] / total[:, HEAD:]).astype(jnp.bfloat16))
        return jnp.concatenate(parts, axis=1)

    lax.fori_loop(0, 2, lambda half, c: (diagonal(half), c)[1], 0)
    for c in three + four:
        c.wait()

    def run(half):
        lax.fori_loop(0, seq, lambda number, c: (earlier(half, number), c)[1], 0)

    run(1 - img)
    other[...] = finish(1 - img)
    columns = pl.ds(pl.multiple_of(img * (OWN_HEADS * HEAD), OWN_HEADS * HEAD), OWN_HEADS * HEAD)
    back = copy(other, out_ref.at[:, columns], 13, partner)
    back.start()
    run(img)
    out_ref[:, columns] = finish(img)
    back.wait()


def attend(rows):
    return pl.pallas_call(
        attend_kernel,
        out_shape=jax.ShapeDtypeStruct((HALF, 2 * OWN_HEADS * HEAD), jnp.bfloat16),
        in_specs=[pl.BlockSpec(memory_space=pltpu.VMEM)],
        out_specs=pl.BlockSpec(memory_space=pltpu.VMEM),
        scratch_shapes=[
            pltpu.VMEM((2, 4, 4, SECTION, HEAD), jnp.bfloat16),
            pltpu.VMEM((8, HEAD), jnp.bfloat16),
            pltpu.VMEM((HALF, OWN_HEADS * HEAD), jnp.bfloat16),
            pltpu.VMEM((2, OWN_HEADS, HALF, HEAD), jnp.float32),
            pltpu.VMEM((2, OWN_HEADS, HALF, 2 * HEAD), jnp.float32),
            pltpu.SemaphoreType.DMA((14,)),
            pltpu.SemaphoreType.DMA((14,)),
        ],
        compiler_params=pltpu.CompilerParams(
            collective_id=0, has_side_effects=True, vmem_limit_bytes=40 * 1024 * 1024
        ),
    )(rows)


def vision(patches, count, vision_gain, vision_shift, vision_qkv, vision_qkv_bias, vision_proj,
           vision_proj_bias, merge_gain, merge_shift, merge_weight, merge_bias):
    source = patches[0].astype(jnp.float32)
    normed_patches = layer_norm(source, vision_gain, vision_shift).astype(jnp.bfloat16)
    local_heads = vision_qkv.shape[1] // (3 * VHEAD)
    mixed = jnp.dot(
        normed_patches, vision_qkv, preferred_element_type=jnp.float32
    ) + vision_qkv_bias.astype(jnp.float32)
    mixed = mixed.astype(jnp.bfloat16).reshape(PATCH_CAP, local_heads, 3, VHEAD)
    scores = jnp.einsum(
        "qhe,khe->hqk", mixed[:, :, 0], mixed[:, :, 1], preferred_element_type=jnp.float32
    )
    scores = scores * VHEAD ** (-0.5)
    valid = jnp.arange(PATCH_CAP, dtype=jnp.int32) < count
    scores = jnp.where(valid[None, None, :], scores, MASKED)
    top_score = jnp.max(scores, axis=-1, keepdims=True)
    raw = jnp.where(valid[None, None, :], jnp.exp(scores - top_score), 0.0)
    totals = jnp.sum(raw, axis=-1)
    context = jnp.einsum(
        "hqk,khe->qhe", raw.astype(jnp.bfloat16), mixed[:, :, 2], preferred_element_type=jnp.float32
    )
    context = (context / jnp.transpose(totals)[:, :, None]).astype(jnp.bfloat16)
    context = context.reshape(PATCH_CAP, local_heads * VHEAD)
    partial_proj = jnp.dot(context, vision_proj, preferred_element_type=jnp.float32)
    summed = lax.psum(partial_proj, ("tp", "img"))
    resid = summed + vision_proj_bias + source
    merge_rows = layer_norm(resid, merge_gain, merge_shift).astype(jnp.bfloat16)
    merge_in = merge_rows.reshape(PATCH_CAP // 4, 4 * VW)
    token_part = jnp.dot(
        merge_in, merge_weight, preferred_element_type=jnp.float32
    ) + merge_bias.astype(jnp.float32)
    return lax.all_gather(token_part.astype(jnp.bfloat16), ("tp", "img"), axis=1, tiled=True)


def on_device(
    patches, patch_counts, image_offsets, vision_gain, vision_shift, vision_qkv, vision_qkv_bias,
    vision_proj, vision_proj_bias, merge_gain, merge_shift, merge_weight, merge_bias, text_embed,
    norm_gain, qkv_weight, qkv_bias,
):
    count = patch_counts[0]
    offset = image_offsets[0]
    img = lax.axis_index("img")
    wide_q = OWN_HEADS * HEAD

    def halves(array):
        first = jnp.concatenate([array[:, :wide_q], array[:, 2 * wide_q : 2 * wide_q + HEAD]], axis=1)
        second = jnp.concatenate([array[:, wide_q : 2 * wide_q], array[:, 2 * wide_q + HEAD :]], axis=1)
        return jnp.stack([first, second])

    shared = lax.all_to_all(halves(qkv_weight), "img", 0, 0)
    weight = lax.all_gather(shared.reshape(-1, shared.shape[-1]), "seq", axis=0, tiled=True)
    bias = halves(qkv_bias[None])[img, 0]
    text = lax.all_gather(lax.all_gather(text_embed, "img", axis=0, tiled=True), "tp", axis=1, tiled=True)
    tokens = vision(
        patches, count, vision_gain, vision_shift, vision_qkv, vision_qkv_bias, vision_proj,
        vision_proj_bias, merge_gain, merge_shift, merge_weight, merge_bias,
    )
    my_start = lax.axis_index("seq") * SECTION
    padded = jnp.pad(tokens, ((SECTION, SECTION), (0, 0)))
    where_at = jnp.clip(my_start - offset + SECTION, 0, PATCH_CAP // 4 + SECTION)
    placed = lax.dynamic_slice_in_dim(padded, where_at, SECTION, 0)
    positions = my_start + jnp.arange(SECTION, dtype=jnp.int32)
    inside = (positions >= offset) & (positions < offset + count // 4)
    hidden = jnp.where(inside[:, None], placed, text)
    wide = hidden.astype(jnp.float32)
    normed = (
        wide
        * lax.rsqrt(jnp.mean(wide * wide, axis=-1, keepdims=True) + EPSILON)
        * norm_gain.astype(jnp.float32)
    ).astype(jnp.bfloat16)
    projected = jnp.dot(normed, weight, preferred_element_type=jnp.float32) + bias.astype(jnp.float32)
    heads = projected.reshape(SECTION, OWN_HEADS + 1, HEAD)
    turned = rotary(heads, positions, HEAD)
    last = jnp.where(img == 0, turned[:, OWN_HEADS:], heads[:, OWN_HEADS:])
    rows = jnp.concatenate([turned[:, :OWN_HEADS], last], axis=1).astype(jnp.bfloat16)
    return attend(rows.reshape(SECTION, (OWN_HEADS + 1) * HEAD))


def solution(mesh):
    placed = (
        P("seq", None, None),
        P("seq"),
        P("seq"),
        P(),
        P(),
        P(None, ("tp", "img")),
        P(("tp", "img")),
        P(("tp", "img"), None),
        P(),
        P(),
        P(),
        P(None, ("tp", "img")),
        P(("tp", "img")),
        P(("seq", "img"), "tp"),
        P(),
        P(("seq", "img"), "tp"),
        P("tp"),
    )
    return jax.shard_map(
        on_device, mesh=mesh, in_specs=placed, out_specs=P(("seq", "img"), "tp"), check_vma=False
    )
```

time: 661 us -> 522 us (0.79)
  waiting for transfers between devices: 460 us -> 333 us
  Pallas kernels: 0 us -> 81.7 us
  matrix products: 104 us -> 35.7 us
  local copies, waits for them, and re-layouts: 27.8 us -> 8.8 us
  blocking collectives: 0 us -> 18 us
  other arithmetic: 40.1 us -> 26.7 us
  loops' own time: 12.2 us -> 0 us
    all_gather x5 -> x4, waiting for transfers between devices: 382 us -> 233 us  [the longest x1 83.1 us: on_device(): lax.all_gather(lax.all_gather(text_embed, 'img', axis=0, tiled=True), 'tp...]
    pallas_call x0 -> x1, Pallas kernels: none -> 81.7 us  [attend(): pl.pallas_call(attend_kernel, out_shape=jax.ShapeDtypeStruct((HALF, 2 * O...]
    dot_general x37 -> x5, matrix products: 98.3 us -> 29.7 us  [the longest x1 13.1 us: on_device(): jnp.dot(normed, weight, preferred_element_type=jnp.float32)]
    psum x1, waiting for transfers between devices: 77.3 us -> 99.5 us  [vision(): summed = lax.psum(partial_proj, ('tp', 'img'))]
    all_to_all x0 -> x1, blocking collectives: none -> 18 us  [on_device(): shared = lax.all_to_all(halves(qkv_weight), 'img', 0, 0)]
    reduce_sum x16 -> x0, other arithmetic: 16.2 us -> none  [compute(): total_new = total_run * factor + jnp.sum(weights, axis=-1)]
    another operation x17 -> x0, loops' own time: 12.2 us -> none  [the longest x1 11 us: on_device(): lax.scan(step_block, initial, (key_blocks, value_blocks, jnp.arange(block...]
    dynamic_slice x16 -> x0, local copies, waits for them, and re-layouts: 9.39 us -> none  [on_device(): lax.scan(step_block, initial, (key_blocks, value_blocks, jnp.arange(block...]
  transfers between devices with their start and end apart: 6 -> 5, of which waited for: 6 -> 4; matrix products, arithmetic and copies ran while one was open for 1% -> 7% of each run, Pallas kernels for 0% -> 0%
where the time goes in v1:
time: 522 us
  waiting for transfers between devices  333 us (64%)
  Pallas kernels  81.7 us (16%)
  matrix products  35.7 us (7%)
  other arithmetic  26.7 us (5%)
  blocking collectives  18 us (3%)
  between operations  16.9 us (3%)
  local copies, waits for them, and re-layouts  8.8 us (2%)
    psum x1, waiting for transfers between devices, vision(): summed = lax.psum(partial_proj, ('tp', 'img'))  99.5 us
    all_gather x1, waiting for transfers between devices, on_device(): lax.all_gather(lax.all_gather(text_embed, 'img', axis=0, tiled=True), 'tp...  83.1 us
    pallas_call x1, Pallas kernels, attend(): pl.pallas_call(attend_kernel, out_shape=jax.ShapeDtypeStruct((HALF, 2 * O...  81.7 us
    all_gather x1, waiting for transfers between devices, vision(): lax.all_gather(token_part.astype(jnp.bfloat16), ('tp', 'img'), axis=1, ti...  77.2 us
    all_gather x1, waiting for transfers between devices, on_device(): lax.all_gather(shared.reshape(-1, shared.shape[-1]), 'seq', axis=0, tiled...  72.4 us
    all_to_all x1, blocking collectives, on_device(): shared = lax.all_to_all(halves(qkv_weight), 'img', 0, 0)  18 us
    dot_general x1, matrix products, on_device(): jnp.dot(normed, weight, preferred_element_type=jnp.float32)  13.1 us
    reduce_sum x1, other arithmetic, on_device(): jnp.mean(wide * wide, axis=-1, keepdims=True) + EPSILON  10.6 us
  transfers between devices with their start and end apart: 5, of which 4 were waited for; matrix products, arithmetic and copies ran while one was open for 7% of the time, Pallas kernels for 0%

profile of v1, /device:TPU:102, one launch (start us, length us, event | category | flops | bytes accessed | tf_op | source)
XLA Modules:
  0.0 521.5 jit_solution(321397885989430345)
XLA Ops:
  8.2 2.5 convert_reduce_fusion
  10.8 2.6 fusion.14
  13.4 1.7 add_convert_fusion.1
  15.1 6.0 %fusion.63 = (f32[2,1024]{1,0:T(2,128)S(1)}, bf16[2,1024,1024]{1,2,0:T(8,128)(2,1)}) fusion(pred[1024]{0:T(1024)(128)(4,1)S(1)} %iota_compare_fusion, bf16[1024,2,3,80]{0,3,2,1:T(8,128)(2,1)S(1)} %bitcast.100), kind=kOutput, calls=%fused_computation.88 | convolution fusion | flops 348128256 | bytes 4859904 | tf_op jit(solution)/shard_map/sub | solution.py:202
  21.1 3.1 fusion.42
  24.2 3.3 fusion.64
  27.6 0.5 all-gather.7.cloned.1.call-update
  28.1 0.2 all-gather.5.cloned.1.call-start
  28.3 99.5 %all-reduce.3.cloned.1.call-done = f32[1024,1280]{1,0:T(8,128)} async-done(((f32[1024,1280]{1,0:T(8,128)}), f32[1024,1280]{1,0:T(8,128)}) %all-reduce.3.cloned.1.call-update) | async-done | bytes 5242896 | tf_op jit(solution)/shard_map/psum | solution.py:210
  127.8 4.2 fusion.31
  132.0 0.5 copy-done.4
  132.6 3.1 multiply_reduce_fusion
  135.7 2.7 add_convert_fusion
  138.4 5.2 %reshape.141 = bf16[256,5120]{1,0:T(8,128)(2,1)} reshape(bf16[1024,1280]{1,0:T(8,128)(2,1)} %add_convert_fusion) | data formatting | bytes 5242880 | tf_op jit(solution)/shard_map/reshape | solution.py:213
  143.6 8.5 %fusion.35 = bf16[256,1024]{1,0:T(8,128)(2,1)} fusion(bf16[256,5120]{1,0:T(8,128)(2,1)} %reshape.141, bf16[5120,1024]{1,0:T(8,128)(2,1)} %param.28, f32[1024]{0:T(1024)S(1)} %convert_element_type.71), kind=kOutput, calls=%fused_computation.42 | convolution fusion | flops 2684878848 | bytes 13635584 | tf_op jit(solution)/shard_map/dot_general | solution.py:214
  152.2 0.0 all-gather.9.cloned.1.call-start
  152.2 0.5 all-gather.9.cloned.1.call-update
  152.9 0.1 maximum_bitcast_fusion
  152.9 0.1 pad_maximum_fusion
  153.0 18.0 %all_to_all.5 = bf16[2,256,640]{2,1,0:T(8,128)(2,1)} all-to-all(bf16[2,256,640]{2,1,0:T(8,128)(2,1)S(1)} %pad_maximum_fusion), channel_id=1, replica_groups=mesh['seq'=16,'tp'=4,'img'=2] {'img'}, dimensions={0} | all-to-all | bytes 1310720 | tf_op jit(solution)/shard_map/all_to_all | solution.py:235
  172.0 0.5 multiply_cosine_fusion
  172.5 77.2 %all-gather.5.cloned.1.call-done = bf16[256,8192]{1,0:T(8,128)(2,1)} async-done(((bf16[256,1024]{1,0:T(8,128)(2,1)}), bf16[256,8192]{1,0:T(8,128)(2,1)}) %all-gather.5.cloned.1.call-update) | async-done | bytes 4194320 | tf_op jit(solution)/shard_map/all_gather | solution.py:217
  249.7 83.1 %all-gather.9.cloned.1.call-done = bf16[512,8192]{1,0:T(8,128)(2,1)} async-done(((bf16[512,2048]{1,0:T(8,128)(2,1)}), bf16[512,8192]{1,0:T(8,128)(2,1)}) %all-gather.9.cloned.1.call-update) | async-done | bytes 8388624 | tf_op jit(solution)/shard_map/all_gather | solution.py:238
  332.8 10.6 %fusion.1 = (f32[512]{0:T(512)S(1)}, bf16[512,8192]{1,0:T(8,128)(2,1)}) fusion(bf16[512,8192]{1,0:T(8,128)(2,1)} %all-gather.9.cloned.1.call-done, s32[]{:T(128)S(6)} %min.4, bf16[256,8192]{1,0:T(8,128)(2,1)} %all-gather.5.cloned.1.call-done, pred[512]{0:T(512)(128)(4,1)S(1)} %fusion.55), kind=kLoop, calls=%fused_computation.4 | loop fusion | flops 16776704 | bytes 20974084 | tf_op jit(solution)/shard_map/reduce_sum | solution.py:253
  343.4 72.4 %all-gather.11.cloned.1.call-done = bf16[8192,640]{1,0:T(8,128)(2,1)} async-done(((bf16[512,640]{1,0:T(8,128)(2,1)}), bf16[8192,640]{1,0:T(8,128)(2,1)}) %all-gather.11.cloned.1.call-update) | async-done | bytes 10485776 | tf_op jit(solution)/shard_map/all_gather | solution.py:236
  415.8 13.1 %fusion.32 = f32[512,640]{1,0:T(8,128)} fusion(bf16[8192,640]{1,0:T(8,128)(2,1)} %all-gather.11.cloned.1.call-done, bf16[512,8192]{1,0:T(8,128)(2,1)} %get-tuple-element.6, f32[8192]{0:T(1024)S(1)} %convert_element_type.74, f32[512]{0:T(512)S(1)} %add_rsqrt_fusion.2, f32[640]{0:T(1024)S(1)} %convert_reduce_fusion.1), kind=kOutput, calls=%fused_computation.38 | convolution fusion | flops 5385814016 | bytes 20222464 | tf_op jit(solution)/shard_map/dot_general | solution.py:256
  428.9 1.8 copy.26
  430.7 0.2 multiply_subtract_fusion
  431.0 0.1 pad_maximum_fusion.1
  431.1 0.3 copy.27.x_ref
  431.4 81.7 %shard_map.163 = bf16[256,1024]{1,0:T(8,128)(2,1)S(1)} custom-call(bf16[512,640]{1,0:T(8,128)(2,1)S(1)} %copy.27.x_ref), custom_call_target="tpu_custom_call" | custom-call | tf_op jit(solution)/shard_map/pallas_call | solution.py:166
  513.1 0.8 copy.36
  (59 shorter events, 0.5 us)
Async XLA Ops:
  7.4 6.0 %copy-start = (bf16[1280,480]{0,1:T(8,128)(2,1)S(1)}, bf16[1280,480]{0,1:T(8,128)(2,1)}, u32[]{:S(2)}) copy-start(bf16[1280,480]{0,1:T(8,128)(2,1)} %param.22) | copy-start | bytes 3686404
  7.4 6.0 %copy-start.13 = (bf16[480]{0:T(512)(128)(2,1)S(1)}, bf16[480]{0:T(512)(128)(2,1)}, u32[]{:S(2)}) copy-start(bf16[480]{0:T(512)(128)(2,1)} %param.23) | copy-start | bytes 2884
  7.4 6.0 %copy-start.15 = (f32[1280]{0:T(1024)S(1)}, f32[1280]{0:T(1024)}, u32[]{:S(2)}) copy-start(f32[1280]{0:T(1024)} %param.20) | copy-start | bytes 15364
  7.4 6.0 %copy-start.14 = (f32[1280]{0:T(1024)S(1)}, f32[1280]{0:T(1024)}, u32[]{:S(2)}) copy-start(f32[1280]{0:T(1024)} %param.21) | copy-start | bytes 15364
  7.4 120.4 %all-reduce.3.cloned.1.call-start = ((), (), s32[]{:S(2)}) async-start(), calls=%async_computation.1 | async-start | bytes 10485760 | tf_op jit(solution)/shard_map/psum | solution.py:210
  7.4 6.0 %copy-start.2 = (bf16[1,1024,1280]{2,1,0:T(8,128)(2,1)S(1)}, bf16[1,1024,1280]{2,1,0:T(8,128)(2,1)}, u32[]{:S(2)}) copy-start(bf16[1,1024,1280]{2,1,0:T(8,128)(2,1)} %param.17) | copy-start | bytes 7864324
  21.1 3.1 copy-start.6
  27.5 0.8 copy-start.12
  27.5 100.3 %copy-start.7 = (f32[1280]{0:T(1024)S(1)}, f32[1280]{0:T(1024)}, u32[]{:S(2)}) copy-start(f32[1280]{0:T(1024)} %param.25) | copy-start | bytes 15364
  27.5 124.7 %all-gather.7.cloned.1.call-start = ((), (), s32[]{:S(2)}) async-start(), calls=%async_computation.3 | async-start | bytes 3145728 | tf_op jit(solution)/shard_map/all_gather | solution.py:238
  28.1 221.6 %all-gather.5.cloned.1.call-start = ((), (), s32[]{:S(2)}) async-start(), calls=%async_computation.2 | async-start | bytes 4718592 | tf_op jit(solution)/shard_map/all_gather | solution.py:217
  127.8 4.8 copy-start.4
  132.0 3.7 copy-start.3
  132.0 3.7 copy-start.9
  132.0 3.7 copy-start.10
  143.6 9.2 %copy-start.5 = (bf16[256,1280]{1,0:T(8,128)(2,1)S(1)}, bf16[256,1280]{1,0:T(8,128)(2,1)}, u32[]{:S(2)}) copy-start(bf16[256,1280]{1,0:T(8,128)(2,1)} %param.32) | copy-start | bytes 1966084
  152.1 19.6 %copy-start.11 = (bf16[1280]{0:T(1024)(128)(2,1)S(1)}, bf16[1280]{0:T(1024)(128)(2,1)}, u32[]{:S(2)}) copy-start(bf16[1280]{0:T(1024)(128)(2,1)} %param.33) | copy-start | bytes 7684
  152.1 19.7 %copy-start.8 = (bf16[8192]{0:T(1024)(128)(2,1)S(1)}, bf16[8192]{0:T(1024)(128)(2,1)}, u32[]{:S(2)}) copy-start(bf16[8192]{0:T(1024)(128)(2,1)} %param.31) | copy-start | bytes 49156
  152.2 180.7 %all-gather.9.cloned.1.call-start = ((), (), s32[]{:S(2)}) async-start(), calls=%async_computation.4 | async-start | bytes 10485760 | tf_op jit(solution)/shard_map/all_gather | solution.py:238
  152.7 263.1 %all-gather.11.cloned.1.call-start = ((), (), s32[]{:S(2)}) async-start(), calls=%async_computation.5 | async-start | bytes 11141120 | tf_op jit(solution)/shard_map/all_gather | solution.py:236
  428.9 85.0 %copy-start.1 = (bf16[1280,480]{0,1:T(8,128)(2,1)S(1)}, bf16[1280,480]{0,1:T(8,128)(2,1)}, u32[]{:S(2)}) copy-start(bf16[1280,480]{0,1:T(8,128)(2,1)} %param.22) | copy-start | bytes 3686404
Sparse Core Ops, SparseCore 0:
  27.6 100.1 all-reduce.2
Sparse Core Ops, SparseCore 1:
  29.6 38.7 all-gather.6
  152.2 97.4 all-gather.4
  251.3 81.5 all-gather.8
  335.0 80.7 all-gather.10

commit v2 on v1

--- a/solution.py
+++ b/solution.py
@@ -21,13 +21,6 @@
 MASKED = -1e30
 LOG2E = 1.4426950408889634
 MESH = pl.DeviceIdType.MESH
-
-
-def layer_norm(source, scaling, shifting):
-    average = jnp.mean(source, axis=-1, keepdims=True)
-    centred = source - average
-    spread = jnp.mean(centred * centred, axis=-1, keepdims=True)
-    return centred * lax.rsqrt(spread + EPSILON) * scaling + shifting
 
 
 def rotary(inputs, positions, head_width):
@@ -183,38 +176,387 @@
     )(rows)
 
 
-def vision(patches, count, vision_gain, vision_shift, vision_qkv, vision_qkv_bias, vision_proj,
-           vision_proj_bias, merge_gain, merge_shift, merge_weight, merge_bias):
-    source = patches[0].astype(jnp.float32)
-    normed_patches = layer_norm(source, vision_gain, vision_shift).astype(jnp.bfloat16)
-    local_heads = vision_qkv.shape[1] // (3 * VHEAD)
-    mixed = jnp.dot(
-        normed_patches, vision_qkv, preferred_element_type=jnp.float32
-    ) + vision_qkv_bias.astype(jnp.float32)
-    mixed = mixed.astype(jnp.bfloat16).reshape(PATCH_CAP, local_heads, 3, VHEAD)
-    scores = jnp.einsum(
-        "qhe,khe->hqk", mixed[:, :, 0], mixed[:, :, 1], preferred_element_type=jnp.float32
-    )
-    scores = scores * VHEAD ** (-0.5)
-    valid = jnp.arange(PATCH_CAP, dtype=jnp.int32) < count
-    scores = jnp.where(valid[None, None, :], scores, MASKED)
-    top_score = jnp.max(scores, axis=-1, keepdims=True)
-    raw = jnp.where(valid[None, None, :], jnp.exp(scores - top_score), 0.0)
-    totals = jnp.sum(raw, axis=-1)
-    context = jnp.einsum(
-        "hqk,khe->qhe", raw.astype(jnp.bfloat16), mixed[:, :, 2], preferred_element_type=jnp.float32
-    )
-    context = (context / jnp.transpose(totals)[:, :, None]).astype(jnp.bfloat16)
-    context = context.reshape(PATCH_CAP, local_heads * VHEAD)
-    partial_proj = jnp.dot(context, vision_proj, preferred_element_type=jnp.float32)
-    summed = lax.psum(partial_proj, ("tp", "img"))
-    resid = summed + vision_proj_bias + source
-    merge_rows = layer_norm(resid, merge_gain, merge_shift).astype(jnp.bfloat16)
-    merge_in = merge_rows.reshape(PATCH_CAP // 4, 4 * VW)
-    token_part = jnp.dot(
-        merge_in, merge_weight, preferred_element_type=jnp.float32
-    ) + merge_bias.astype(jnp.float32)
-    return lax.all_gather(token_part.astype(jnp.bfloat16), ("tp", "img"), axis=1, tiled=True)
+def ring_gather(copy, base, block, part, here, ahead, behind):
+    before, after = (here + 3) % 4, (here + 1) % 4
+    send_up = copy(block(here), block(here), base, ahead)
+    send_down = copy(block(here), block(here), base + 1, behind)
+    pass_up = copy(part(before, 0), part(before, 0), base + 2, ahead)
+    pass_down = copy(part(after, 1), part(after, 1), base + 3, behind)
+
+    def start():
+        send_up.start()
+        send_down.start()
+
+    def turn():
+        send_up.wait_recv()
+        pass_up.start()
+        send_down.wait_recv()
+        pass_down.start()
+
+    def done():
+        pass_up.wait_recv()
+        pass_down.wait_recv()
+        for c in (send_up, send_down, pass_up, pass_down):
+            c.wait_send()
+
+    return start, turn, done
+
+
+def column_gather(copy, base, slot, part, y, core, device):
+    before, after, far = (y + 3) % 4, (y + 1) % 4, (y + 2) % 4
+    ahead, behind, sibling = device(after, core), device(before, core), device(y, 1 - core)
+    own = slot(y, core)
+    share = copy(own, own, base, sibling)
+    send_up = copy(own, own, base + 1, ahead)
+    send_down = copy(own, own, base + 2, behind)
+    low, high = part(before, core, 0), part(after, core, 1)
+    pass_up = copy(low, low, base + 3, ahead)
+    pass_down = copy(high, high, base + 4, behind)
+    left, right = slot(before, core), slot(after, core)
+    give_left = copy(left, left, base + 5, sibling)
+    give_right = copy(right, right, base + 6, sibling)
+    far_low, far_high = part(far, core, 0), part(far, core, 1)
+    give_low = copy(far_low, far_low, base + 7, sibling)
+    give_high = copy(far_high, far_high, base + 8, sibling)
+
+    def start():
+        send_up.start()
+        send_down.start()
+        share.start()
+
+    def turn():
+        send_up.wait_recv()
+        pass_up.start()
+        give_left.start()
+        send_down.wait_recv()
+        pass_down.start()
+        give_right.start()
+
+    def last():
+        pass_up.wait_recv()
+        give_low.start()
+        pass_down.wait_recv()
+        give_high.start()
+
+    def done():
+        for c in (share, give_left, give_right, give_low, give_high):
+            c.wait_recv()
+        for c in (share, send_up, send_down, pass_up, pass_down, give_left, give_right, give_low, give_high):
+            c.wait_send()
+
+    return start, turn, last, done
+
+
+def vision_kernel(
+    count_ref, patches_ref, gain_ref, shift_ref, qkv_ref, qkv_bias_ref, proj_ref, proj_bias_ref,
+    merge_gain_ref, merge_shift_ref, merge_ref, merge_bias_ref, text_ref, norm_gain_ref, half_ref,
+    text_out, vision_out,
+    mixed, ctx, ctx_in, proj_all, merge_w, lines, merge_in, tok, weight, text, squares,
+    send, recv, ctx_send, ctx_recv, local,
+):
+    seq = lax.axis_index("seq")
+    tp = lax.axis_index("tp")
+    img = lax.axis_index("img")
+    x, z = seq // 4, seq % 4
+    core, y = tp % 2, img * 2 + tp // 2
+    me = tp * 2 + img
+
+    def device(y_at, core_at):
+        return {"tp": 2 * (y_at % 2) + core_at, "img": y_at // 2}
+
+    def order(y_at, core_at):
+        return (2 * (y_at % 2) + core_at) * 2 + y_at // 2
+
+    def along_x(d):
+        return {"seq": ((x + d) % 4) * 4 + z}
+
+    def along_z(d):
+        return {"seq": x * 4 + (z + d) % 4}
+
+    def member(index):
+        return {"tp": index // 2, "img": index % 2}
+
+    peers = [member((me + d) % 8) for d in range(1, 8)]
+    peers += [along_x(1), along_x(3), along_z(1), along_z(3)]
+    barrier = pltpu.get_barrier_semaphore()
+    for peer in peers:
+        pl.semaphore_signal(barrier, inc=1, device_id=peer, device_id_type=MESH)
+    load_merge = pltpu.make_async_copy(merge_ref, merge_w, local.at[0])
+    load_merge.start()
+    load_half = pltpu.make_async_copy(half_ref.at[img], weight.at[x, z, img], local.at[1])
+    load_half.start()
+    load_text = pltpu.make_async_copy(text_ref, text.at[tp, img], local.at[2])
+    load_text.start()
+    proj_all[:, 2 * VHEAD :, :] = jnp.zeros((8, 256 - 2 * VHEAD, VW), jnp.bfloat16)
+    proj_all[me, : 2 * VHEAD, :] = proj_ref[...]
+    pl.semaphore_wait(barrier, len(peers))
+
+    def copy(src, dst, number, peer):
+        return pltpu.make_async_remote_copy(
+            src_ref=src,
+            dst_ref=dst,
+            send_sem=send.at[number],
+            recv_sem=recv.at[number],
+            device_id=peer,
+            device_id_type=MESH,
+        )
+
+    proj_gather = column_gather(
+        copy, 0,
+        lambda a, b: proj_all.at[order(a, b), pl.ds(0, 160)],
+        lambda a, b, h: proj_all.at[order(a, b), pl.ds(80 * h, 80)],
+        y, core, device,
+    )
+    merge_gather = column_gather(
+        copy, 9,
+        lambda a, b: merge_in.at[:, pl.ds(order(a, b) * 32, 32)],
+        lambda a, b, h: merge_in.at[pl.ds(2 * h, 2), pl.ds(order(a, b) * 32, 32)],
+        y, core, device,
+    )
+    token_gather = column_gather(
+        copy, 18,
+        lambda a, b: tok.at[order(a, b)],
+        lambda a, b, h: tok.at[order(a, b), pl.ds(128 * h, 128)],
+        y, core, device,
+    )
+    text_gather = column_gather(
+        copy, 27,
+        lambda a, b: text.at[2 * (a % 2) + b, a // 2],
+        lambda a, b, h: text.at[2 * (a % 2) + b, a // 2, pl.ds(128 * h, 128)],
+        y, core, device,
+    )
+    swap_src = half_ref.at[1 - img]
+    swap = copy(swap_src, weight.at[x, z, img], 36, {"img": 1 - img})
+    theirs = 1 - img
+    one_x = ring_gather(
+        copy, 37,
+        lambda a: weight.at[a, z, img],
+        lambda a, h: weight.at[a, z, img, pl.ds(128 * h, 128)],
+        x, along_x(1), along_x(3),
+    )
+    one_z = ring_gather(
+        copy, 41,
+        lambda a: weight.at[x, a, theirs],
+        lambda a, h: weight.at[x, a, theirs, pl.ds(128 * h, 128)],
+        z, along_z(1), along_z(3),
+    )
+    two_z = ring_gather(
+        copy, 45,
+        lambda a: weight.at[:, a, img],
+        lambda a, h: weight.at[:, a, img, pl.ds(128 * h, 128)],
+        z, along_z(1), along_z(3),
+    )
+    two_x = ring_gather(
+        copy, 49,
+        lambda a: weight.at[a, :, theirs],
+        lambda a, h: weight.at[a, :, theirs, pl.ds(128 * h, 128)],
+        x, along_x(1), along_x(3),
+    )
+
+    proj_gather[0]()
+    swap.start()
+    load_half.wait()
+    one_x[0]()
+
+    def norm(source, gain, shift):
+        average = jnp.mean(source, axis=-1, keepdims=True)
+        centred = source - average
+        spread = jnp.mean(centred * centred, axis=-1, keepdims=True)
+        return centred * lax.rsqrt(spread + EPSILON) * gain + shift
+
+    def mix(number, carry):
+        rows = pl.ds(number * 256, 256)
+        normed = norm(patches_ref[rows, :].astype(jnp.float32), gain_ref[...], shift_ref[...])
+        product = jnp.dot(normed.astype(jnp.bfloat16), qkv_ref[...], preferred_element_type=jnp.float32)
+        mixed[rows, :] = (product + qkv_bias_ref[...]).astype(jnp.bfloat16)
+        return carry
+
+    lax.fori_loop(0, 4, mix, 0)
+    proj_gather[1]()
+    swap.wait()
+    one_z[0]()
+    one_x[1]()
+    valid = lax.broadcasted_iota(jnp.int32, (256, PATCH_CAP), 1) < count_ref[0]
+    lane = lax.broadcasted_iota(jnp.int32, (256, HEAD), 1)
+
+    def look(number):
+        rows = pl.ds(number * 256, 256)
+        parts = []
+        for head in range(2):
+            query = mixed[rows, 384 * head : 384 * head + 128]
+            keys = mixed[:, 384 * head + 128 : 384 * head + 256]
+            values = mixed[:, 384 * head + 256 : 384 * head + 384]
+            scores = lax.dot_general(
+                query, keys, (((1,), (1,)), ((), ())), preferred_element_type=jnp.float32
+            )
+            scores = jnp.where(valid, scores * (VHEAD ** (-0.5) * LOG2E), MASKED)
+            best = jnp.max(scores, axis=-1, keepdims=True)
+            weights = jnp.exp2(scores - best).astype(jnp.bfloat16)
+            product = jnp.dot(weights, values, preferred_element_type=jnp.float32)
+            parts.append(product / product[:, VHEAD : VHEAD + 1])
+        turned = pltpu.roll(parts[1], VHEAD, 1)
+        ctx[rows, :HEAD] = jnp.where(lane < VHEAD, parts[0], turned).astype(jnp.bfloat16)
+        ctx[rows, HEAD:] = jnp.where(lane < 2 * VHEAD - HEAD, turned, 0.0).astype(jnp.bfloat16)
+
+    def ctx_copy(number, target):
+        return pltpu.make_async_remote_copy(
+            src_ref=ctx.at[pl.ds(target * 128, 128)],
+            dst_ref=ctx_in.at[me],
+            send_sem=ctx_send.at[number],
+            recv_sem=ctx_recv.at[me],
+            device_id=member(target),
+            device_id_type=MESH,
+        )
+
+    pair = me // 2
+    def look_step(number, carry):
+        target = (pair + 1 + number) % 4
+        look(target)
+        ctx_copy(2 * number, 2 * target).start()
+        ctx_copy(2 * number + 1, 2 * target + 1).start()
+        return carry
+
+    lax.fori_loop(0, 3, look_step, 0)
+    look(pair)
+    ctx_copy(6, 2 * pair + 1 - img).start()
+    ctx_in[me] = ctx[pl.ds(me * 128, 128), :]
+    one_z[1]()
+    one_x[2]()
+    two_z[0]()
+    proj_gather[2]()
+    proj_gather[3]()
+    one_z[2]()
+    two_x[0]()
+
+    def arrived(number, carry):
+        source = (me + 1 + number) % 8
+        pltpu.make_async_remote_copy(
+            src_ref=ctx.at[pl.ds(0, 128)],
+            dst_ref=ctx_in.at[source],
+            send_sem=ctx_send.at[number],
+            recv_sem=ctx_recv.at[source],
+            device_id=member(source),
+            device_id_type=MESH,
+        ).wait()
+        return carry
+
+    lax.fori_loop(0, 7, arrived, 0)
+    resid = patches_ref[pl.ds(me * 128, 128), :].astype(jnp.float32) + proj_bias_ref[...]
+    for number in range(8):
+        resid = resid + jnp.dot(ctx_in[number], proj_all[number], preferred_element_type=jnp.float32)
+    settled = norm(resid, merge_gain_ref[...], merge_shift_ref[...])
+    for tile in range(VW // HEAD):
+        lines[tile] = settled[:, tile * HEAD : (tile + 1) * HEAD]
+    for number in range(4):
+        picked = [lines[tile, pl.ds(number, 32, stride=4), :] for tile in range(VW // HEAD)]
+        merge_in[number, pl.ds(me * 32, 32), :] = jnp.concatenate(picked, axis=1).astype(jnp.bfloat16)
+    merge_gather[0]()
+    load_text.wait()
+    merge_gather[1]()
+    merge_gather[2]()
+    load_merge.wait()
+    merge_gather[3]()
+
+    def merge(number, carry):
+        columns = pl.ds(pl.multiple_of(number * 256, 256), 256)
+        total = merge_bias_ref[:, columns]
+        for part in range(4):
+            total = total + jnp.dot(
+                merge_in[part], merge_w[pl.ds(part * VW, VW), columns], preferred_element_type=jnp.float32
+            )
+        tok[me, :, columns] = total.astype(jnp.bfloat16)
+        return carry
+
+    lax.fori_loop(0, 4, merge, 0)
+    token_gather[0]()
+    text_gather[0]()
+    two_z[1]()
+    two_x[1]()
+    token_gather[1]()
+    text_gather[1]()
+    token_gather[2]()
+    text_gather[2]()
+    two_z[2]()
+    two_x[2]()
+    token_gather[3]()
+
+    def weigh(rows, wide, chunk, first):
+        scaled = (wide * norm_gain_ref[chunk]).astype(jnp.bfloat16)
+        folded = jnp.zeros((256, HEAD), jnp.float32)
+        for number in range(8):
+            piece = wide[:, number * HEAD : (number + 1) * HEAD]
+            folded = folded + piece * piece
+        w = weight[chunk // 2, pl.ds((chunk % 2) * 2, 2)].reshape(1024, 5 * HEAD)
+        return jnp.dot(scaled, w, preferred_element_type=jnp.float32), folded
+
+    def vision_step(chunk, carry):
+        product, folded = weigh(None, tok[chunk].astype(jnp.float32), chunk, None)
+        vision_out[...] += product
+        squares[0] += folded
+        return carry
+
+    def text_step(chunk, carry):
+        for half in range(2):
+            columns = pl.ds(pl.multiple_of((chunk % 2) * 1024, 1024), 1024)
+            wide = text[chunk // 2, half, :, columns].astype(jnp.float32)
+            product, folded = weigh(None, wide, chunk, None)
+            text_out[half] += product
+            squares[1 + half] += folded
+        return carry
+
+    squares[...] = jnp.zeros_like(squares)
+    vision_out[...] = jnp.zeros_like(vision_out)
+    text_out[...] = jnp.zeros_like(text_out)
+    lax.fori_loop(0, 8, vision_step, 0)
+    text_gather[3]()
+    lax.fori_loop(0, 8, text_step, 0)
+
+    def scale(number):
+        mean = jnp.sum(squares[number], axis=-1, keepdims=True) * (1.0 / 8192)
+        return lax.rsqrt(mean + EPSILON)
+
+    vision_out[...] = vision_out[...] * scale(0)
+    text_out[0] = text_out[0] * scale(1)
+    text_out[1] = text_out[1] * scale(2)
+
+
+def encode(count, patches, gain, shift, qkv, qkv_bias, proj, proj_bias, merge_gain, merge_shift,
+           merge_weight, merge_bias, text, norm_gain, half):
+    vmem = pl.BlockSpec(memory_space=pltpu.VMEM)
+    hbm = pl.BlockSpec(memory_space=pl.ANY)
+    smem = pl.BlockSpec(memory_space=pltpu.SMEM)
+    bf16, f32 = jnp.bfloat16, jnp.float32
+    return pl.pallas_call(
+        vision_kernel,
+        out_shape=(
+            jax.ShapeDtypeStruct((2, 256, 5 * HEAD), f32),
+            jax.ShapeDtypeStruct((256, 5 * HEAD), f32),
+        ),
+        in_specs=[smem] + [vmem] * 9 + [hbm] + [vmem] + [hbm] + [vmem] + [hbm],
+        out_specs=(vmem, vmem),
+        scratch_shapes=[
+            pltpu.VMEM((PATCH_CAP, 6 * HEAD), bf16),
+            pltpu.VMEM((PATCH_CAP, 2 * HEAD), bf16),
+            pltpu.VMEM((8, 128, 2 * HEAD), bf16),
+            pltpu.VMEM((8, 256, VW), bf16),
+            pltpu.VMEM((4 * VW, 1024), bf16),
+            pltpu.VMEM((VW // HEAD, 128, HEAD), f32),
+            pltpu.VMEM((4, 256, VW), bf16),
+            pltpu.VMEM((8, 256, 1024), bf16),
+            pltpu.VMEM((4, 4, 2, 256, 5 * HEAD), bf16),
+            pltpu.VMEM((4, 2, 256, 2048), bf16),
+            pltpu.VMEM((3, 256, HEAD), f32),
+            pltpu.SemaphoreType.DMA((53,)),
+            pltpu.SemaphoreType.DMA((53,)),
+            pltpu.SemaphoreType.DMA((7,)),
+            pltpu.SemaphoreType.DMA((8,)),
+            pltpu.SemaphoreType.DMA((3,)),
+        ],
+        compiler_params=pltpu.CompilerParams(
+            collective_id=1, has_side_effects=True, vmem_limit_bytes=62 * 1024 * 1024
+        ),
+    )(count, patches, gain, shift, qkv, qkv_bias, proj, proj_bias, merge_gain, merge_shift,
+      merge_weight, merge_bias, text, norm_gain, half)
 
 
 def on_device(
@@ -226,34 +568,32 @@
     offset = image_offsets[0]
     img = lax.axis_index("img")
     wide_q = OWN_HEADS * HEAD
+    f32 = jnp.float32
 
     def halves(array):
         first = jnp.concatenate([array[:, :wide_q], array[:, 2 * wide_q : 2 * wide_q + HEAD]], axis=1)
         second = jnp.concatenate([array[:, wide_q : 2 * wide_q], array[:, 2 * wide_q + HEAD :]], axis=1)
         return jnp.stack([first, second])
 
-    shared = lax.all_to_all(halves(qkv_weight), "img", 0, 0)
-    weight = lax.all_gather(shared.reshape(-1, shared.shape[-1]), "seq", axis=0, tiled=True)
+    spare = ((0, 0), (0, 0), (0, HEAD - VHEAD))
+    wide_qkv = jnp.pad(vision_qkv.reshape(VW, 6, VHEAD), spare).reshape(VW, 6 * HEAD)
+    wide_bias = jnp.pad(vision_qkv_bias.astype(f32).reshape(1, 6, VHEAD), spare)
+    wide_bias = wide_bias.at[:, 2::3, VHEAD].set(1.0).reshape(1, 6 * HEAD)
+    from_text, from_vision = encode(
+        patch_counts, patches[0], vision_gain[None], vision_shift[None], wide_qkv, wide_bias,
+        vision_proj, vision_proj_bias[None], merge_gain[None], merge_shift[None], merge_weight,
+        merge_bias.astype(f32)[None], text_embed, norm_gain.astype(f32).reshape(8, 1, 1024),
+        halves(qkv_weight),
+    )
+    from_text = from_text.reshape(SECTION, 5 * HEAD)
     bias = halves(qkv_bias[None])[img, 0]
-    text = lax.all_gather(lax.all_gather(text_embed, "img", axis=0, tiled=True), "tp", axis=1, tiled=True)
-    tokens = vision(
-        patches, count, vision_gain, vision_shift, vision_qkv, vision_qkv_bias, vision_proj,
-        vision_proj_bias, merge_gain, merge_shift, merge_weight, merge_bias,
-    )
     my_start = lax.axis_index("seq") * SECTION
-    padded = jnp.pad(tokens, ((SECTION, SECTION), (0, 0)))
+    padded = jnp.pad(from_vision, ((SECTION, SECTION), (0, 0)))
     where_at = jnp.clip(my_start - offset + SECTION, 0, PATCH_CAP // 4 + SECTION)
     placed = lax.dynamic_slice_in_dim(padded, where_at, SECTION, 0)
     positions = my_start + jnp.arange(SECTION, dtype=jnp.int32)
     inside = (positions >= offset) & (positions < offset + count // 4)
-    hidden = jnp.where(inside[:, None], placed, text)
-    wide = hidden.astype(jnp.float32)
-    normed = (
-        wide
-        * lax.rsqrt(jnp.mean(wide * wide, axis=-1, keepdims=True) + EPSILON)
-        * norm_gain.astype(jnp.float32)
-    ).astype(jnp.bfloat16)
-    projected = jnp.dot(normed, weight, preferred_element_type=jnp.float32) + bias.astype(jnp.float32)
+    projected = jnp.where(inside[:, None], placed, from_text) + bias.astype(f32)
     heads = projected.reshape(SECTION, OWN_HEADS + 1, HEAD)
     turned = rotary(heads, positions, HEAD)
     last = jnp.where(img == 0, turned[:, OWN_HEADS:], heads[:, OWN_HEADS:])

time: 522 us -> 225 us (0.43)
  waiting for transfers between devices: 333 us -> 0 us
  Pallas kernels: 81.7 us -> 208 us
  matrix products: 35.7 us -> 0 us
  other arithmetic: 26.7 us -> 4.92 us
  blocking collectives: 18 us -> 0 us
  between operations: 16.9 us -> 1.58 us
    all_gather x4 -> x0, waiting for transfers between devices: 233 us -> none  [the longest x1 83.1 us: on_device(): lax.all_gather(lax.all_gather(text_embed, 'img', axis=0, tiled=True), 'tp...]
    pallas_call x0 -> x1, Pallas kernels: none -> 128 us  [encode(): pl.pallas_call(vision_kernel, out_shape=(jax.ShapeDtypeStruct((2, 256, 5...]
    psum x1 -> x0, waiting for transfers between devices: 99.5 us -> none  [vision(): summed = lax.psum(partial_proj, ('tp', 'img'))]
    dot_general x5 -> x0, matrix products: 29.7 us -> none  [the longest x1 13.1 us: on_device(): jnp.dot(normed, weight, preferred_element_type=jnp.float32)]
    reduce_sum x5 -> x0, other arithmetic: 22.9 us -> none  [the longest x1 10.6 us: on_device(): jnp.mean(wide * wide, axis=-1, keepdims=True) + EPSILON]
    all_to_all x1 -> x0, blocking collectives: 18 us -> none  [on_device(): shared = lax.all_to_all(halves(qkv_weight), 'img', 0, 0)]
    sub x1 -> x0, matrix products: 5.99 us -> none  [vision(): raw = jnp.where(valid[None, None, :], jnp.exp(scores - top_score), 0.0)]
  transfers between devices with their start and end apart: 5 -> 0, of which waited for: 4 -> 0; matrix products, arithmetic and copies ran while one was open for 7% -> 0% of each run, Pallas kernels for 0% -> 0%
where the time goes in v2:
time: 225 us
  Pallas kernels  208 us (92%)
  local copies, waits for them, and re-layouts  11.1 us (5%)
  other arithmetic  4.92 us (2%)
    pallas_call x1, Pallas kernels, encode(): pl.pallas_call(vision_kernel, out_shape=(jax.ShapeDtypeStruct((2, 256, 5...  128 us
    pallas_call x1, Pallas kernels, attend(): pl.pallas_call(attend_kernel, out_shape=jax.ShapeDtypeStruct((HALF, 2 * O...  79.1 us

profile of v2, /device:TPU:102, one launch (start us, length us, event | category | flops | bytes accessed | tf_op | source)
XLA Modules:
  0.0 225.1 jit_solution(14468842706694358171)
XLA Ops:
  1.3 1.3 broadcast_in_dim.37.gain_ref
  2.6 1.3 broadcast_in_dim.38.shift_ref
  3.9 1.4 pad.16
  5.3 0.0 copy-start.7
  5.3 0.0 copy-start.2
  5.3 0.0 copy-start.3
  5.3 0.0 copy-start.4
  5.4 0.0 copy-start.6
  5.4 0.0 copy-start.1
  5.4 0.0 copy-start
  5.4 2.4 %copy.19.qkv_ref = bf16[1280,768]{1,0:T(8,128)(2,1)} copy(bf16[1280,768]{0,1:T(8,128)(2,1)S(1)} %bitcast.37) | data formatting | bytes 3932160 | tf_op jit(solution)/shard_map/reshape | solution.py:579
  7.7 0.0 copy-done.7
  7.8 0.1 reshape.113
  7.9 0.6 scatter_fusion
  8.5 0.6 copy.24
  9.1 0.6 broadcast_in_dim.39.proj_bias_ref
  9.7 0.6 broadcast_in_dim.40.merge_gain_ref
  10.3 0.0 copy-done.4
  10.3 0.6 broadcast_in_dim.41.merge_shift_ref
  10.9 0.6 broadcast_in_dim.45
  11.5 0.6 reshape.120
  12.2 0.1 maximum_bitcast_fusion
  12.2 0.9 pad_maximum_fusion.half_ref
  13.2 128.5 %shard_map.163 = (f32[2,256,640]{2,1,0:T(8,128)}, f32[256,640]{1,0:T(8,128)}) custom-call(s32[1]{0:T(128)} %copy.27.count_ref, bf16[1024,1280]{1,0:T(8,128)(2,1)} %bitcast.41, f32[1,1280]{1,0:T(1,128)} %broadcast_in_dim.37.gain_ref, f32[1,1280]{1,0:T(1,128)} %broadcast_in_dim.38.shift_ref, bf16[1280,768]{1,0:T(8,128)(2,1)} %copy.19.qkv_ref, ...), custom_call_target="tpu_custom_call" | custom-call | tf_op jit(solution)/shard_map/pallas_call | solution.py:529
  141.8 1.8 fusion.1
  143.6 0.4 copy.20
  144.0 0.5 multiply_cosine_fusion
  144.6 0.2 multiply_subtract_fusion
  144.9 0.1 pad_maximum_fusion.1
  144.9 0.3 copy.21.x_ref
  145.2 79.1 %shard_map.164 = bf16[256,1024]{1,0:T(8,128)(2,1)S(1)} custom-call(bf16[512,640]{1,0:T(8,128)(2,1)S(1)} %copy.21.x_ref), custom_call_target="tpu_custom_call" | custom-call | tf_op jit(solution)/shard_map/pallas_call | solution.py:159
  224.3 0.8 copy.29
  (22 shorter events, 0.2 us)
Async XLA Ops:
  5.3 2.4 %copy-start.7 = (bf16[480]{0:T(512)(128)(2,1)S(1)}, bf16[480]{0:T(512)(128)(2,1)}, u32[]{:S(2)}) copy-start(bf16[480]{0:T(512)(128)(2,1)} %param.23) | copy-start | bytes 2884
  5.3 3.8 %copy-start.2 = (f32[1280]{0:T(1024)S(1)}, f32[1280]{0:T(1024)}, u32[]{:S(2)}) copy-start(f32[1280]{0:T(1024)} %param.25) | copy-start | bytes 15364
  5.3 4.4 %copy-start.3 = (f32[1280]{0:T(1024)S(1)}, f32[1280]{0:T(1024)}, u32[]{:S(2)}) copy-start(f32[1280]{0:T(1024)} %param.26) | copy-start | bytes 15364
  5.3 5.0 %copy-start.4 = (f32[1280]{0:T(1024)S(1)}, f32[1280]{0:T(1024)}, u32[]{:S(2)}) copy-start(f32[1280]{0:T(1024)} %param.27) | copy-start | bytes 15364
  5.4 5.5 %copy-start.6 = (bf16[1024]{0:T(1024)(128)(2,1)S(1)}, bf16[1024]{0:T(1024)(128)(2,1)}, u32[]{:S(2)}) copy-start(bf16[1024]{0:T(1024)(128)(2,1)} %param.29) | copy-start | bytes 6148
  5.4 6.1 %copy-start.1 = (bf16[8192]{0:T(1024)(128)(2,1)S(1)}, bf16[8192]{0:T(1024)(128)(2,1)}, u32[]{:S(2)}) copy-start(bf16[8192]{0:T(1024)(128)(2,1)} %param.31) | copy-start | bytes 49156
  5.4 6.7 %copy-start = (bf16[256,1280]{1,0:T(8,128)(2,1)S(1)}, bf16[256,1280]{1,0:T(8,128)(2,1)}, u32[]{:S(2)}) copy-start(bf16[256,1280]{1,0:T(8,128)(2,1)} %param.32) | copy-start | bytes 1966084
  13.2 128.5 %copy-start.5 = (bf16[1280]{0:T(1024)(128)(2,1)S(1)}, bf16[1280]{0:T(1024)(128)(2,1)}, u32[]{:S(2)}) copy-start(bf16[1280]{0:T(1024)(128)(2,1)} %param.33) | copy-start | bytes 7684

commit v3 on v2

--- a/solution.py
+++ b/solution.py
@@ -40,12 +40,108 @@
     )
 
 
-def attend_kernel(x_ref, out_ref, buf, ext, other, top, acc, send, recv):
+def ring_gather(copy, base, block, part, here, ahead, behind):
+    before, after = (here + 3) % 4, (here + 1) % 4
+    send_up = copy(block(here), block(here), base, ahead)
+    send_down = copy(block(here), block(here), base + 1, behind)
+    pass_up = copy(part(before, 0), part(before, 0), base + 2, ahead)
+    pass_down = copy(part(after, 1), part(after, 1), base + 3, behind)
+
+    def start():
+        send_up.start()
+        send_down.start()
+
+    def turn():
+        send_up.wait_recv()
+        pass_up.start()
+        send_down.wait_recv()
+        pass_down.start()
+
+    def done():
+        pass_up.wait_recv()
+        pass_down.wait_recv()
+        for c in (send_up, send_down, pass_up, pass_down):
+            c.wait_send()
+
+    return start, turn, done
+
+
+def grid_gather(copy, base, block, part, first, second, ahead, behind):
+    before, after, far = (first + 3) % 4, (first + 1) % 4, (first + 2) % 4
+    low, high = (second + 3) % 4, (second + 1) % 4
+
+    def whole(number, a, way):
+        return copy(block(a, second), block(a, second), base + number, way)
+
+    def half(number, a, b, h, way):
+        return copy(part(a, b, h), part(a, b, h), base + number, way)
+
+    up, down = whole(0, first, ahead[0]), whole(1, first, behind[0])
+    pass_up = half(2, before, second, 0, ahead[0])
+    pass_down = half(3, after, second, 1, behind[0])
+    columns = (first, before, after, far)
+    over = [(whole(4 + 2 * n, a, ahead[1]), whole(5 + 2 * n, a, behind[1])) for n, a in enumerate(columns)]
+    on = [
+        (half(12 + 2 * n, a, low, 0, ahead[1]), half(13 + 2 * n, a, high, 1, behind[1]))
+        for n, a in enumerate(columns)
+    ]
+
+    def spread(n):
+        over[n][0].start()
+        over[n][1].start()
+
+    def relay(n):
+        over[n][0].wait_recv()
+        on[n][0].start()
+        over[n][1].wait_recv()
+        on[n][1].start()
+
+    def begin():
+        up.start()
+        down.start()
+        spread(0)
+
+    def turn():
+        up.wait_recv()
+        pass_up.start()
+        spread(1)
+        down.wait_recv()
+        pass_down.start()
+        spread(2)
+
+    def near():
+        relay(0)
+
+    def turned():
+        pass_up.wait_recv()
+        pass_down.wait_recv()
+        spread(3)
+
+    def middle():
+        relay(1)
+        relay(2)
+
+    def last():
+        relay(3)
+
+    def done():
+        for c in on:
+            c[0].wait_recv()
+            c[1].wait_recv()
+        for c in [(up, down), (pass_up, pass_down)] + over + on:
+            c[0].wait_send()
+            c[1].wait_send()
+
+    return begin, turn, near, turned, middle, last, done
+
+
+def attend_kernel(x_ref, out_ref, buf, guest, query, away, home, top, acc, send, recv):
     seq = lax.axis_index("seq")
     img = lax.axis_index("img")
     x = seq // 4
     z = seq % 4
     partner = {"img": 1 - img}
+    mirror = 15 - seq
 
     def along_x(d):
         return {"seq": ((x + d) % 4) * 4 + z}
@@ -53,105 +149,122 @@
     def along_z(d):
         return {"seq": x * 4 + (z + d) % 4}
 
-    peers = [partner] + [along_x(d) for d in (1, 2, 3)] + [along_z(d) for d in (1, 2, 3)]
+    peers = [partner, along_x(1), along_x(3), along_z(1), along_z(3)]
+    peers += [{"seq": mirror}, {"seq": mirror, "img": 1 - img}]
     barrier = pltpu.get_barrier_semaphore()
     for peer in peers:
         pl.semaphore_signal(barrier, inc=1, device_id=peer, device_id_type=MESH)
-    pl.semaphore_wait(barrier, len(peers))
-
-    def copy(src, dst, number, peer):
+
+    def remote(src, dst, out, into, peer):
         return pltpu.make_async_remote_copy(
             src_ref=src,
             dst_ref=dst,
-            send_sem=send.at[number],
-            recv_sem=recv.at[number],
+            send_sem=send.at[out],
+            recv_sem=recv.at[into],
             device_id=peer,
             device_id_type=MESH,
         )
 
-    buf[img, x, z] = x_ref[:, OWN_HEADS * HEAD :]
-    own = buf.at[img, x, z]
-    swap = copy(own, own, 0, partner)
+    def copy(src, dst, number, peer):
+        return remote(src, dst, number, number, peer)
+
+    two = 2 * HEAD
+    own_rows = x_ref[:, OWN_HEADS * HEAD :].astype(jnp.float32)
+    flipped = [own_rows[n * HEAD : (n + 1) * HEAD].T for n in range(SECTION // HEAD)]
+    buf[img, x, z] = jnp.where(img == 0, jnp.concatenate(flipped, axis=0), own_rows).astype(jnp.bfloat16)
+    pl.semaphore_wait(barrier, len(peers))
+    swap = copy(buf.at[img, x, z], buf.at[img, x, z], 0, partner)
     swap.start()
-    swap.wait()
+    lend = copy(x_ref.at[:, pl.ds(two, two)], guest, 1, {"seq": mirror})
+    lend.start()
     first, second = pl.ds(0, HALF), pl.ds(HALF, HALF)
-    part_a = buf.at[:, x, z, first]
-    part_b = buf.at[:, x, z, second]
-    one = [copy(part_a, part_a, d, along_x(d)) for d in (1, 2, 3)]
-    two = [copy(part_b, part_b, 3 + d, along_z(d)) for d in (1, 2, 3)]
-    for c in one + two:
-        c.start()
-    for c in one:
-        c.wait()
-    part_c = buf.at[:, :, z, first]
-    three = [copy(part_c, part_c, 6 + d, along_z(d)) for d in (1, 2, 3)]
-    for c in three:
-        c.start()
-    for c in two:
-        c.wait()
-    part_d = buf.at[:, x, :, second]
-    four = [copy(part_d, part_d, 9 + d, along_x(d)) for d in (1, 2, 3)]
-    for c in four:
-        c.start()
-
+    ways = (along_x(1), along_z(1)), (along_x(3), along_z(3))
+    gather_one = grid_gather(
+        copy, 2,
+        lambda a, b: buf.at[:, a, b, first],
+        lambda a, b, h: buf.at[h, a, b, first],
+        x, z, ways[0], ways[1],
+    )
+    gather_two = grid_gather(
+        copy, 22,
+        lambda a, b: buf.at[:, b, a, second],
+        lambda a, b, h: buf.at[h, b, a, second],
+        z, x, ways[0][::-1], ways[1][::-1],
+    )
     top[...] = jnp.full_like(top, MASKED)
     acc[...] = jnp.zeros_like(acc)
+    for head in range(2):
+        query[pl.ds(head * SECTION, SECTION), :] = x_ref[:, head * HEAD : (head + 1) * HEAD]
+    rows_all = 2 * SECTION
     ones = jnp.ones((SECTION, HEAD), jnp.bfloat16)
-
-    def block(half, rows, head, keys, values, mask):
-        query = x_ref[rows, head * HEAD : (head + 1) * HEAD]
-        scores = lax.dot_general(
-            query, keys, (((1,), (1,)), ((), ())), preferred_element_type=jnp.float32
-        )
+    tiles = SECTION // HEAD
+
+    def block(group, number, masked):
+        rows = pl.ds(group * rows_all, rows_all)
+        a, b = number // 4, number % 4
+        keys = jnp.concatenate([buf[0, a, b, n * HEAD : (n + 1) * HEAD] for n in range(tiles)], axis=1)
+        values = jnp.concatenate([buf[1, a, b], ones], axis=1)
+        scores = jnp.dot(query[rows, :], keys, preferred_element_type=jnp.float32)
         scores = scores * (HEAD ** (-0.5) * LOG2E)
-        if mask is not None:
-            scores = jnp.where(mask, scores, MASKED)
-        old = top[half, head]
+        if masked:
+            row = lax.broadcasted_iota(jnp.int32, (rows_all, SECTION), 0) % SECTION
+            col = lax.broadcasted_iota(jnp.int32, (rows_all, SECTION), 1)
+            scores = jnp.where(col <= row, scores, MASKED)
+        old = top[rows, :]
         new = jnp.maximum(old, jnp.max(scores, axis=-1, keepdims=True))
         factor = jnp.exp2(old - new)
-        weights = jnp.exp2(scores - new[:, :1]).astype(jnp.bfloat16)
+        weights = [jnp.exp2(scores[:, n * HEAD : (n + 1) * HEAD] - new) for n in range(tiles)]
+        weights = jnp.concatenate(weights, axis=1).astype(jnp.bfloat16)
         product = jnp.dot(weights, values, preferred_element_type=jnp.float32)
-        top[half, head] = new
-        acc[half, head] = acc[half, head] * jnp.concatenate([factor, factor], axis=1) + product
-
-    def diagonal(half):
-        rows = pl.ds(half * HALF, HALF)
-        keys = buf[0, x, z]
-        values = jnp.concatenate([buf[1, x, z], ones], axis=1)
-        row = lax.broadcasted_iota(jnp.int32, (HALF, SECTION), 0) + half * HALF
-        col = lax.broadcasted_iota(jnp.int32, (HALF, SECTION), 1)
-        mask = col <= row
-        for head in range(OWN_HEADS):
-            block(half, rows, head, keys, values, mask)
-
-    def earlier(half, number):
-        rows = pl.ds(half * HALF, HALF)
-        keys = buf[0, number // 4, number % 4]
-        values = jnp.concatenate([buf[1, number // 4, number % 4], ones], axis=1)
-        for head in range(OWN_HEADS):
-            block(half, rows, head, keys, values, None)
-
-    def finish(half):
+        top[rows, :] = new
+        acc[rows, :] = acc[rows, :] * jnp.concatenate([factor, factor], axis=1) + product
+
+    def run(group, count):
+        lax.fori_loop(0, count, lambda number, c: (block(group, number, False), c)[1], 0)
+
+    def finish(group):
         parts = []
-        for head in range(OWN_HEADS):
-            total = acc[half, head]
+        for head in range(2):
+            total = acc[pl.ds(group * rows_all + head * SECTION, SECTION), :]
             parts.append((total[:, :HEAD] / total[:, HEAD:]).astype(jnp.bfloat16))
         return jnp.concatenate(parts, axis=1)
 
-    lax.fori_loop(0, 2, lambda half, c: (diagonal(half), c)[1], 0)
-    for c in three + four:
-        c.wait()
-
-    def run(half):
-        lax.fori_loop(0, seq, lambda number, c: (earlier(half, number), c)[1], 0)
-
-    run(1 - img)
-    other[...] = finish(1 - img)
-    columns = pl.ds(pl.multiple_of(img * (OWN_HEADS * HEAD), OWN_HEADS * HEAD), OWN_HEADS * HEAD)
-    back = copy(other, out_ref.at[:, columns], 13, partner)
+    swap.wait()
+    gather_one[0]()
+    gather_two[0]()
+    block(0, seq, True)
+    for step in range(1, 7):
+        gather_one[step]()
+        gather_two[step]()
+    lend.wait()
+    for head in range(2):
+        query[pl.ds(rows_all + head * SECTION, SECTION), :] = guest[:, head * HEAD : (head + 1) * HEAD]
+    block(1, mirror, True)
+    run(1, mirror)
+    away[...] = finish(1)
+    to_mirror = [
+        remote(
+            away.at[pl.ds(HALF * n, HALF)],
+            out_ref.at[:, pl.ds(pl.multiple_of(img * 2 * two + two, two), two)],
+            42 + n, 42 + img, {"seq": mirror, "img": n},
+        )
+        for n in range(2)
+    ]
+    for c in to_mirror:
+        c.start()
+    run(0, seq)
+    home[...] = finish(0)
+    columns = pl.ds(pl.multiple_of(img * 2 * two, two), two)
+    back = copy(home.at[pl.ds(pl.multiple_of((1 - img) * HALF, HALF), HALF)], out_ref.at[:, columns], 44, partner)
     back.start()
-    run(img)
-    out_ref[:, columns] = finish(img)
+    out_ref[:, columns] = home[pl.ds(pl.multiple_of(img * HALF, HALF), HALF), :]
+    for n in range(2):
+        to_mirror[n].wait_send()
+        remote(
+            away.at[pl.ds(HALF * n, HALF)],
+            out_ref.at[:, pl.ds(n * 2 * two + two, two)],
+            42 + n, 42 + n, {"seq": mirror, "img": n},
+        ).wait_recv()
     back.wait()
 
 
@@ -163,43 +276,19 @@
         out_specs=pl.BlockSpec(memory_space=pltpu.VMEM),
         scratch_shapes=[
             pltpu.VMEM((2, 4, 4, SECTION, HEAD), jnp.bfloat16),
-            pltpu.VMEM((8, HEAD), jnp.bfloat16),
-            pltpu.VMEM((HALF, OWN_HEADS * HEAD), jnp.bfloat16),
-            pltpu.VMEM((2, OWN_HEADS, HALF, HEAD), jnp.float32),
-            pltpu.VMEM((2, OWN_HEADS, HALF, 2 * HEAD), jnp.float32),
-            pltpu.SemaphoreType.DMA((14,)),
-            pltpu.SemaphoreType.DMA((14,)),
+            pltpu.VMEM((SECTION, 2 * HEAD), jnp.bfloat16),
+            pltpu.VMEM((4 * SECTION, HEAD), jnp.bfloat16),
+            pltpu.VMEM((SECTION, 2 * HEAD), jnp.bfloat16),
+            pltpu.VMEM((SECTION, 2 * HEAD), jnp.bfloat16),
+            pltpu.VMEM((4 * SECTION, HEAD), jnp.float32),
+            pltpu.VMEM((4 * SECTION, 2 * HEAD), jnp.float32),
+            pltpu.SemaphoreType.DMA((45,)),
+            pltpu.SemaphoreType.DMA((45,)),
         ],
         compiler_params=pltpu.CompilerParams(
             collective_id=0, has_side_effects=True, vmem_limit_bytes=40 * 1024 * 1024
         ),
     )(rows)
-
-
-def ring_gather(copy, base, block, part, here, ahead, behind):
-    before, after = (here + 3) % 4, (here + 1) % 4
-    send_up = copy(block(here), block(here), base, ahead)
-    send_down = copy(block(here), block(here), base + 1, behind)
-    pass_up = copy(part(before, 0), part(before, 0), base + 2, ahead)
-    pass_down = copy(part(after, 1), part(after, 1), base + 3, behind)
-
-    def start():
-        send_up.start()
-        send_down.start()
-
-    def turn():
-        send_up.wait_recv()
-        pass_up.start()
-        send_down.wait_recv()
-        pass_down.start()
-
-    def done():
-        pass_up.wait_recv()
-        pass_down.wait_recv()
-        for c in (send_up, send_down, pass_up, pass_down):
-            c.wait_send()
-
-    return start, turn, done
 
 
 def column_gather(copy, base, slot, part, y, core, device):

time: 225 us -> 205 us (0.911); the launches traced: 225 us -> 203 us
  Pallas kernels: 208 us -> 185 us
    pallas_call x1, Pallas kernels: 79.1 us -> 56.7 us  [attend(): pl.pallas_call(attend_kernel, out_shape=jax.ShapeDtypeStruct((HALF, 2 * O...]
where the time goes in v3:
time: 205 us; the launch traced here: 203 us
  Pallas kernels  185 us (90%)
  local copies, waits for them, and re-layouts  11.1 us (5%)
  other arithmetic  4.92 us (2%)
    pallas_call x1, Pallas kernels, encode(): pl.pallas_call(vision_kernel, out_shape=(jax.ShapeDtypeStruct((2, 256, 5...  129 us
    pallas_call x1, Pallas kernels, attend(): pl.pallas_call(attend_kernel, out_shape=jax.ShapeDtypeStruct((HALF, 2 * O...  56.7 us

profile of v3, /device:TPU:102, one launch (start us, length us, event | category | flops | bytes accessed | tf_op | source)
XLA Modules:
  0.0 202.9 jit_solution(12151111325929474704)
XLA Ops:
  1.3 1.3 broadcast_in_dim.37.gain_ref
  2.6 1.3 broadcast_in_dim.38.shift_ref
  3.9 1.4 pad.16
  5.3 0.0 copy-start.7
  5.3 0.0 copy-start.2
  5.3 0.0 copy-start.3
  5.3 0.0 copy-start.4
  5.4 0.0 copy-start.6
  5.4 0.0 copy-start.1
  5.4 0.0 copy-start
  5.4 2.4 %copy.19.qkv_ref = bf16[1280,768]{1,0:T(8,128)(2,1)} copy(bf16[1280,768]{0,1:T(8,128)(2,1)S(1)} %bitcast.37) | data formatting | bytes 3932160 | tf_op jit(solution)/shard_map/reshape | solution.py:668
  7.7 0.0 copy-done.7
  7.8 0.1 reshape.113
  7.9 0.6 scatter_fusion
  8.5 0.6 copy.24
  9.1 0.6 broadcast_in_dim.39.proj_bias_ref
  9.7 0.6 broadcast_in_dim.40.merge_gain_ref
  10.3 0.0 copy-done.4
  10.3 0.6 broadcast_in_dim.41.merge_shift_ref
  10.9 0.6 broadcast_in_dim.45
  11.5 0.6 reshape.120
  12.2 0.1 maximum_bitcast_fusion
  12.2 0.9 pad_maximum_fusion.half_ref
  13.2 128.7 %shard_map.163 = (f32[2,256,640]{2,1,0:T(8,128)}, f32[256,640]{1,0:T(8,128)}) custom-call(s32[1]{0:T(128)} %copy.27.count_ref, bf16[1024,1280]{1,0:T(8,128)(2,1)} %bitcast.41, f32[1,1280]{1,0:T(1,128)} %broadcast_in_dim.37.gain_ref, f32[1,1280]{1,0:T(1,128)} %broadcast_in_dim.38.shift_ref, bf16[1280,768]{1,0:T(8,128)(2,1)} %copy.19.qkv_ref, ...), custom_call_target="tpu_custom_call" | custom-call | tf_op jit(solution)/shard_map/pallas_call | solution.py:618
  142.0 1.8 fusion.1
  143.8 0.4 copy.20
  144.2 0.5 multiply_cosine_fusion
  144.7 0.2 multiply_subtract_fusion
  145.0 0.1 pad_maximum_fusion.1
  145.1 0.3 copy.21.x_ref
  145.4 56.7 %shard_map.164 = bf16[256,1024]{1,0:T(8,128)(2,1)S(1)} custom-call(bf16[512,640]{1,0:T(8,128)(2,1)S(1)} %copy.21.x_ref), custom_call_target="tpu_custom_call" | custom-call | tf_op jit(solution)/shard_map/pallas_call | solution.py:272
  202.1 0.8 copy.29
  (22 shorter events, 0.2 us)
Async XLA Ops:
  5.3 2.4 %copy-start.7 = (bf16[480]{0:T(512)(128)(2,1)S(1)}, bf16[480]{0:T(512)(128)(2,1)}, u32[]{:S(2)}) copy-start(bf16[480]{0:T(512)(128)(2,1)} %param.23) | copy-start | bytes 2884
  5.3 3.8 %copy-start.2 = (f32[1280]{0:T(1024)S(1)}, f32[1280]{0:T(1024)}, u32[]{:S(2)}) copy-start(f32[1280]{0:T(1024)} %param.25) | copy-start | bytes 15364
  5.3 4.4 %copy-start.3 = (f32[1280]{0:T(1024)S(1)}, f32[1280]{0:T(1024)}, u32[]{:S(2)}) copy-start(f32[1280]{0:T(1024)} %param.26) | copy-start | bytes 15364
  5.3 5.0 %copy-start.4 = (f32[1280]{0:T(1024)S(1)}, f32[1280]{0:T(1024)}, u32[]{:S(2)}) copy-start(f32[1280]{0:T(1024)} %param.27) | copy-start | bytes 15364
  5.4 5.5 %copy-start.6 = (bf16[1024]{0:T(1024)(128)(2,1)S(1)}, bf16[1024]{0:T(1024)(128)(2,1)}, u32[]{:S(2)}) copy-start(bf16[1024]{0:T(1024)(128)(2,1)} %param.29) | copy-start | bytes 6148
  5.4 6.1 %copy-start.1 = (bf16[8192]{0:T(1024)(128)(2,1)S(1)}, bf16[8192]{0:T(1024)(128)(2,1)}, u32[]{:S(2)}) copy-start(bf16[8192]{0:T(1024)(128)(2,1)} %param.31) | copy-start | bytes 49156
  5.4 6.7 %copy-start = (bf16[256,1280]{1,0:T(8,128)(2,1)S(1)}, bf16[256,1280]{1,0:T(8,128)(2,1)}, u32[]{:S(2)}) copy-start(bf16[256,1280]{1,0:T(8,128)(2,1)} %param.32) | copy-start | bytes 1966084
  13.2 128.7 %copy-start.5 = (bf16[1280]{0:T(1024)(128)(2,1)S(1)}, bf16[1280]{0:T(1024)(128)(2,1)}, u32[]{:S(2)}) copy-start(bf16[1280]{0:T(1024)(128)(2,1)} %param.33) | copy-start | bytes 7684

commit v4 on v3

--- a/solution.py
+++ b/solution.py
@@ -23,47 +23,11 @@
 MESH = pl.DeviceIdType.MESH
 
 
-def rotary(inputs, positions, head_width):
-    halfway = head_width // 2
-    frequency = jnp.power(
-        jnp.float32(THETA), -(jnp.arange(halfway, dtype=jnp.float32) * 2.0) / head_width
-    )
+def rotation(positions):
+    halfway = HEAD // 2
+    frequency = jnp.power(jnp.float32(THETA), -(jnp.arange(halfway, dtype=jnp.float32) * 2.0) / HEAD)
     angles = positions.astype(jnp.float32)[:, None] * frequency[None, :]
-    angles = angles.reshape((angles.shape[0],) + (1,) * (inputs.ndim - 2) + (halfway,))
-    cosine = jnp.cos(angles)
-    sine_value = jnp.sin(angles)
-    leading = inputs[..., :halfway]
-    trailing = inputs[..., halfway:]
-    return jnp.concatenate(
-        [leading * cosine - trailing * sine_value, trailing * cosine + leading * sine_value],
-        axis=-1,
-    )
-
-
-def ring_gather(copy, base, block, part, here, ahead, behind):
-    before, after = (here + 3) % 4, (here + 1) % 4
-    send_up = copy(block(here), block(here), base, ahead)
-    send_down = copy(block(here), block(here), base + 1, behind)
-    pass_up = copy(part(before, 0), part(before, 0), base + 2, ahead)
-    pass_down = copy(part(after, 1), part(after, 1), base + 3, behind)
-
-    def start():
-        send_up.start()
-        send_down.start()
-
-    def turn():
-        send_up.wait_recv()
-        pass_up.start()
-        send_down.wait_recv()
-        pass_down.start()
-
-    def done():
-        pass_up.wait_recv()
-        pass_down.wait_recv()
-        for c in (send_up, send_down, pass_up, pass_down):
-            c.wait_send()
-
-    return start, turn, done
+    return jnp.cos(angles), jnp.sin(angles)
 
 
 def grid_gather(copy, base, block, part, first, second, ahead, behind):
@@ -337,10 +301,9 @@
 
 
 def vision_kernel(
-    count_ref, patches_ref, gain_ref, shift_ref, qkv_ref, qkv_bias_ref, proj_ref, proj_bias_ref,
-    merge_gain_ref, merge_shift_ref, merge_ref, merge_bias_ref, text_ref, norm_gain_ref, half_ref,
-    text_out, vision_out,
-    mixed, ctx, ctx_in, proj_all, merge_w, lines, merge_in, tok, weight, text, squares,
+    count_ref, start_ref, patches_ref, rows_ref, turn_ref, qkv_ref, proj_ref, merge_ref, text_ref, part_ref,
+    rows_out,
+    wide, mixed, flipped, ctx, ctx_in, proj_all, merge_w, lines, merge_in, weight, text, hidden, total, squares,
     send, recv, ctx_send, ctx_recv, local,
 ):
     seq = lax.axis_index("seq")
@@ -349,6 +312,7 @@
     x, z = seq // 4, seq % 4
     core, y = tp % 2, img * 2 + tp // 2
     me = tp * 2 + img
+    gain, shift, proj_bias, merge_gain, merge_shift = [rows_ref[n : n + 1, :] for n in range(5)]
 
     def device(y_at, core_at):
         return {"tp": 2 * (y_at % 2) + core_at, "img": y_at // 2}
@@ -372,9 +336,22 @@
         pl.semaphore_signal(barrier, inc=1, device_id=peer, device_id_type=MESH)
     load_merge = pltpu.make_async_copy(merge_ref, merge_w, local.at[0])
     load_merge.start()
-    load_half = pltpu.make_async_copy(half_ref.at[img], weight.at[x, z, img], local.at[1])
-    load_half.start()
-    load_text = pltpu.make_async_copy(text_ref, text.at[tp, img], local.at[2])
+    kept = [(img * 512, 0, 512), (1024 + img * HEAD, 512, HEAD)]
+    given = [((1 - img) * 512, 0, 512), (1024 + (1 - img) * HEAD, 512, HEAD)]
+
+    mine = pl.ds(pl.multiple_of(img * 1024, 1024), 1024)
+    yours = pl.ds(pl.multiple_of((1 - img) * 1024, 1024), 1024)
+
+    def columns_of(start, size):
+        return part_ref.at[:, pl.ds(pl.multiple_of(start, HEAD), size)]
+
+    load_half = [
+        pltpu.make_async_copy(columns_of(at, size), weight.at[x, z, img, :, pl.ds(to, size)], local.at[1 + n])
+        for n, (at, to, size) in enumerate(kept)
+    ]
+    for c in load_half:
+        c.start()
+    load_text = pltpu.make_async_copy(text_ref.at[:, mine], text.at[img], local.at[3])
     load_text.start()
     proj_all[:, 2 * VHEAD :, :] = jnp.zeros((8, 256 - 2 * VHEAD, VW), jnp.bfloat16)
     proj_all[me, : 2 * VHEAD, :] = proj_ref[...]
@@ -402,85 +379,90 @@
         lambda a, b, h: merge_in.at[pl.ds(2 * h, 2), pl.ds(order(a, b) * 32, 32)],
         y, core, device,
     )
-    token_gather = column_gather(
-        copy, 18,
-        lambda a, b: tok.at[order(a, b)],
-        lambda a, b, h: tok.at[order(a, b), pl.ds(128 * h, 128)],
-        y, core, device,
-    )
-    text_gather = column_gather(
-        copy, 27,
-        lambda a, b: text.at[2 * (a % 2) + b, a // 2],
-        lambda a, b, h: text.at[2 * (a % 2) + b, a // 2, pl.ds(128 * h, 128)],
-        y, core, device,
-    )
-    swap_src = half_ref.at[1 - img]
-    swap = copy(swap_src, weight.at[x, z, img], 36, {"img": 1 - img})
+    hidden_gather = [
+        column_gather(
+            copy, 18 + 9 * n,
+            lambda a, b, n=n: hidden.at[order(a, b), n],
+            lambda a, b, h, n=n: hidden.at[order(a, b), n, pl.ds(256 * h, 256)],
+            y, core, device,
+        )
+        for n in range(4)
+    ]
+    text_swap = [
+        copy(text_ref.at[pl.ds(128 * n, 128), yours], text.at[img, pl.ds(128 * n, 128)], 54 + n, {"img": 1 - img})
+        for n in range(2)
+    ]
+    swap = [
+        copy(columns_of(at, size), weight.at[x, z, img, :, pl.ds(to, size)], 56 + n, {"img": 1 - img})
+        for n, (at, to, size) in enumerate(given)
+    ]
     theirs = 1 - img
-    one_x = ring_gather(
-        copy, 37,
-        lambda a: weight.at[a, z, img],
-        lambda a, h: weight.at[a, z, img, pl.ds(128 * h, 128)],
-        x, along_x(1), along_x(3),
-    )
-    one_z = ring_gather(
-        copy, 41,
-        lambda a: weight.at[x, a, theirs],
-        lambda a, h: weight.at[x, a, theirs, pl.ds(128 * h, 128)],
-        z, along_z(1), along_z(3),
-    )
-    two_z = ring_gather(
-        copy, 45,
-        lambda a: weight.at[:, a, img],
-        lambda a, h: weight.at[:, a, img, pl.ds(128 * h, 128)],
-        z, along_z(1), along_z(3),
-    )
-    two_x = ring_gather(
-        copy, 49,
-        lambda a: weight.at[a, :, theirs],
-        lambda a, h: weight.at[a, :, theirs, pl.ds(128 * h, 128)],
-        x, along_x(1), along_x(3),
+    ways = (along_x(1), along_z(1)), (along_x(3), along_z(3))
+    weight_one = grid_gather(
+        copy, 58,
+        lambda a, b: weight.at[a, b, img],
+        lambda a, b, h: weight.at[a, b, img, pl.ds(128 * h, 128)],
+        x, z, ways[0], ways[1],
+    )
+    weight_two = grid_gather(
+        copy, 78,
+        lambda a, b: weight.at[b, a, theirs],
+        lambda a, b, h: weight.at[b, a, theirs, pl.ds(128 * h, 128)],
+        z, x, ways[0][::-1], ways[1][::-1],
     )
 
     proj_gather[0]()
-    swap.start()
-    load_half.wait()
-    one_x[0]()
-
-    def norm(source, gain, shift):
+    for c in load_half:
+        c.wait()
+    weight_one[0]()
+    for c in swap:
+        c.start()
+
+    def norm(source, scaling, shifting):
         average = jnp.mean(source, axis=-1, keepdims=True)
         centred = source - average
         spread = jnp.mean(centred * centred, axis=-1, keepdims=True)
-        return centred * lax.rsqrt(spread + EPSILON) * gain + shift
+        return centred * lax.rsqrt(spread + EPSILON) * scaling + shifting
+
+    old = lax.broadcasted_iota(jnp.int32, (6 * VHEAD, 6 * HEAD), 0)
+    new = lax.broadcasted_iota(jnp.int32, (6 * VHEAD, 6 * HEAD), 1)
+    place = ((old // VHEAD == new // HEAD) & (old % VHEAD == new % HEAD)).astype(jnp.float32).astype(jnp.bfloat16)
+    wide[...] = jnp.dot(qkv_ref[...], place, preferred_element_type=jnp.float32).astype(jnp.bfloat16)
+    bias = jnp.dot(
+        rows_ref[5:6, : 6 * VHEAD].astype(jnp.bfloat16), place, preferred_element_type=jnp.float32
+    )
+    column = lax.broadcasted_iota(jnp.int32, (1, 6 * HEAD), 1)
+    bias = bias + ((column % HEAD == VHEAD) & ((column // HEAD) % 3 == 2)).astype(jnp.float32)
 
     def mix(number, carry):
-        rows = pl.ds(number * 256, 256)
-        normed = norm(patches_ref[rows, :].astype(jnp.float32), gain_ref[...], shift_ref[...])
-        product = jnp.dot(normed.astype(jnp.bfloat16), qkv_ref[...], preferred_element_type=jnp.float32)
-        mixed[rows, :] = (product + qkv_bias_ref[...]).astype(jnp.bfloat16)
+        rows = pl.ds(pl.multiple_of(number * 512, 512), 512)
+        normed = norm(patches_ref[rows, :].astype(jnp.float32), gain, shift)
+        product = jnp.dot(normed.astype(jnp.bfloat16), wide[...], preferred_element_type=jnp.float32) + bias
+        mixed[rows, :] = product.astype(jnp.bfloat16)
+        for head in range(2):
+            keys = product[:, 384 * head + 128 : 384 * head + 256].T
+            flipped[head, :, rows] = keys.astype(jnp.bfloat16)
         return carry
 
-    lax.fori_loop(0, 4, mix, 0)
-    proj_gather[1]()
-    swap.wait()
-    one_z[0]()
-    one_x[1]()
-    valid = lax.broadcasted_iota(jnp.int32, (256, PATCH_CAP), 1) < count_ref[0]
-    lane = lax.broadcasted_iota(jnp.int32, (256, HEAD), 1)
+    lax.fori_loop(0, 2, mix, 0)
+    for c in swap:
+        c.wait()
+    weight_two[0]()
+    weight_one[1]()
+    valid = lax.broadcasted_iota(jnp.int32, (512, PATCH_CAP), 1) < count_ref[0]
+    lane = lax.broadcasted_iota(jnp.int32, (512, HEAD), 1)
 
     def look(number):
-        rows = pl.ds(number * 256, 256)
+        rows = pl.ds(pl.multiple_of(number * 512, 512), 512)
         parts = []
         for head in range(2):
             query = mixed[rows, 384 * head : 384 * head + 128]
-            keys = mixed[:, 384 * head + 128 : 384 * head + 256]
             values = mixed[:, 384 * head + 256 : 384 * head + 384]
-            scores = lax.dot_general(
-                query, keys, (((1,), (1,)), ((), ())), preferred_element_type=jnp.float32
-            )
+            scores = jnp.dot(query, flipped[head], preferred_element_type=jnp.float32)
             scores = jnp.where(valid, scores * (VHEAD ** (-0.5) * LOG2E), MASKED)
-            best = jnp.max(scores, axis=-1, keepdims=True)
-            weights = jnp.exp2(scores - best).astype(jnp.bfloat16)
+            best = jnp.max(scores, axis=-1, keepdims=True) + jnp.zeros((512, HEAD), jnp.float32)
+            weights = [jnp.exp2(scores[:, n * HEAD : (n + 1) * HEAD] - best) for n in range(8)]
+            weights = jnp.concatenate(weights, axis=1).astype(jnp.bfloat16)
             product = jnp.dot(weights, values, preferred_element_type=jnp.float32)
             parts.append(product / product[:, VHEAD : VHEAD + 1])
         turned = pltpu.roll(parts[1], VHEAD, 1)
@@ -489,7 +471,7 @@
 
     def ctx_copy(number, target):
         return pltpu.make_async_remote_copy(
-            src_ref=ctx.at[pl.ds(target * 128, 128)],
+            src_ref=ctx.at[pl.ds(pl.multiple_of(target * 128, 128), 128)],
             dst_ref=ctx_in.at[me],
             send_sem=ctx_send.at[number],
             recv_sem=ctx_recv.at[me],
@@ -497,25 +479,20 @@
             device_id_type=MESH,
         )
 
-    pair = me // 2
-    def look_step(number, carry):
-        target = (pair + 1 + number) % 4
-        look(target)
-        ctx_copy(2 * number, 2 * target).start()
-        ctx_copy(2 * number + 1, 2 * target + 1).start()
-        return carry
-
-    lax.fori_loop(0, 3, look_step, 0)
-    look(pair)
-    ctx_copy(6, 2 * pair + 1 - img).start()
-    ctx_in[me] = ctx[pl.ds(me * 128, 128), :]
-    one_z[1]()
-    one_x[2]()
-    two_z[0]()
+    side = me // 4
+    look(1 - side)
+    for n in range(4):
+        ctx_copy(n, (1 - side) * 4 + n).start()
+    proj_gather[1]()
+    look(side)
+    for n in range(3):
+        ctx_copy(4 + n, side * 4 + (me + 1 + n) % 4).start()
+    ctx_in[me] = ctx[pl.ds(pl.multiple_of(me * 128, 128), 128), :]
     proj_gather[2]()
-    proj_gather[3]()
-    one_z[2]()
-    two_x[0]()
+    text_swap[0].start()
+    weight_two[1]()
+    weight_one[2]()
+    weight_two[2]()
 
     def arrived(number, carry):
         source = (me + 1 + number) % 8
@@ -530,122 +507,129 @@
         return carry
 
     lax.fori_loop(0, 7, arrived, 0)
-    resid = patches_ref[pl.ds(me * 128, 128), :].astype(jnp.float32) + proj_bias_ref[...]
+    proj_gather[3]()
+    resid = patches_ref[pl.ds(me * 128, 128), :].astype(jnp.float32) + proj_bias
     for number in range(8):
         resid = resid + jnp.dot(ctx_in[number], proj_all[number], preferred_element_type=jnp.float32)
-    settled = norm(resid, merge_gain_ref[...], merge_shift_ref[...])
+    settled = norm(resid, merge_gain, merge_shift)
     for tile in range(VW // HEAD):
         lines[tile] = settled[:, tile * HEAD : (tile + 1) * HEAD]
     for number in range(4):
         picked = [lines[tile, pl.ds(number, 32, stride=4), :] for tile in range(VW // HEAD)]
         merge_in[number, pl.ds(me * 32, 32), :] = jnp.concatenate(picked, axis=1).astype(jnp.bfloat16)
     merge_gather[0]()
+    weight_one[3]()
+    weight_two[3]()
+    load_merge.wait()
+    merge_gather[1]()
+    weight_one[4]()
+    weight_two[4]()
+    merge_gather[2]()
+    text_swap[1].start()
     load_text.wait()
-    merge_gather[1]()
-    merge_gather[2]()
-    load_merge.wait()
+    first = start_ref[0] - seq * SECTION
+    spot = lax.broadcasted_iota(jnp.int32, (SECTION, 256), 0) - first
+    slot = lax.broadcasted_iota(jnp.int32, (SECTION, 256), 1)
+    pick = ((spot == slot) & (slot < count_ref[0] // 4)).astype(jnp.float32).astype(jnp.bfloat16)
     merge_gather[3]()
-
-    def merge(number, carry):
-        columns = pl.ds(pl.multiple_of(number * 256, 256), 256)
-        total = merge_bias_ref[:, columns]
+    for c in text_swap:
+        c.wait()
+    spot = lax.broadcasted_iota(jnp.int32, (SECTION, 256), 0) - first
+    inside = (spot >= 0) & (spot < count_ref[0] // 4)
+    for number in range(4):
+        if number == 2:
+            weight_one[5]()
+            weight_two[5]()
+        columns = slice(256 * number, 256 * number + 256)
+        token = rows_ref[6:7, columns]
         for part in range(4):
-            total = total + jnp.dot(
-                merge_in[part], merge_w[pl.ds(part * VW, VW), columns], preferred_element_type=jnp.float32
+            token = token + jnp.dot(
+                merge_in[part], merge_w[part * VW : part * VW + VW, columns], preferred_element_type=jnp.float32
             )
-        tok[me, :, columns] = total.astype(jnp.bfloat16)
-        return carry
-
-    lax.fori_loop(0, 4, merge, 0)
-    token_gather[0]()
-    text_gather[0]()
-    two_z[1]()
-    two_x[1]()
-    token_gather[1]()
-    text_gather[1]()
-    token_gather[2]()
-    text_gather[2]()
-    two_z[2]()
-    two_x[2]()
-    token_gather[3]()
-
-    def weigh(rows, wide, chunk, first):
-        scaled = (wide * norm_gain_ref[chunk]).astype(jnp.bfloat16)
-        folded = jnp.zeros((256, HEAD), jnp.float32)
+        placed = jnp.dot(pick, token.astype(jnp.bfloat16), preferred_element_type=jnp.float32)
+        words = text[:, :, columns].reshape(SECTION, 256).astype(jnp.float32)
+        hidden[me, number] = jnp.where(inside, placed, words).astype(jnp.bfloat16)
+        hidden_gather[number][0]()
+    squares[...] = jnp.zeros_like(squares)
+    total[...] = jnp.zeros_like(total)
+
+    def weigh(chunk):
+        values = jnp.concatenate([hidden[chunk, n] for n in range(4)], axis=1).astype(jnp.float32)
+        scaled = (values * rows_ref[pl.ds(8 + chunk, 1), :1024]).astype(jnp.bfloat16)
+        folded = jnp.zeros((SECTION, HEAD), jnp.float32)
         for number in range(8):
-            piece = wide[:, number * HEAD : (number + 1) * HEAD]
+            piece = values[:, number * HEAD : (number + 1) * HEAD]
             folded = folded + piece * piece
         w = weight[chunk // 2, pl.ds((chunk % 2) * 2, 2)].reshape(1024, 5 * HEAD)
-        return jnp.dot(scaled, w, preferred_element_type=jnp.float32), folded
-
-    def vision_step(chunk, carry):
-        product, folded = weigh(None, tok[chunk].astype(jnp.float32), chunk, None)
-        vision_out[...] += product
-        squares[0] += folded
+        total[...] += jnp.dot(scaled, w, preferred_element_type=jnp.float32)
+        squares[...] += folded
+
+    for number in range(4):
+        hidden_gather[number][1]()
+    weight_one[6]()
+    weight_two[6]()
+    weigh(me)
+    for number in range(4):
+        hidden_gather[number][2]()
+    weigh(order((y + 1) % 4, core))
+    weigh(order((y + 3) % 4, core))
+    for number in range(4):
+        hidden_gather[number][3]()
+    weigh(order((y + 2) % 4, core))
+
+    def rest(number, carry):
+        weigh(order((y + number) % 4, 1 - core))
         return carry
 
-    def text_step(chunk, carry):
-        for half in range(2):
-            columns = pl.ds(pl.multiple_of((chunk % 2) * 1024, 1024), 1024)
-            wide = text[chunk // 2, half, :, columns].astype(jnp.float32)
-            product, folded = weigh(None, wide, chunk, None)
-            text_out[half] += product
-            squares[1 + half] += folded
-        return carry
-
-    squares[...] = jnp.zeros_like(squares)
-    vision_out[...] = jnp.zeros_like(vision_out)
-    text_out[...] = jnp.zeros_like(text_out)
-    lax.fori_loop(0, 8, vision_step, 0)
-    text_gather[3]()
-    lax.fori_loop(0, 8, text_step, 0)
-
-    def scale(number):
-        mean = jnp.sum(squares[number], axis=-1, keepdims=True) * (1.0 / 8192)
-        return lax.rsqrt(mean + EPSILON)
-
-    vision_out[...] = vision_out[...] * scale(0)
-    text_out[0] = text_out[0] * scale(1)
-    text_out[1] = text_out[1] * scale(2)
-
-
-def encode(count, patches, gain, shift, qkv, qkv_bias, proj, proj_bias, merge_gain, merge_shift,
-           merge_weight, merge_bias, text, norm_gain, half):
+    lax.fori_loop(0, 4, rest, 0)
+    scale = lax.rsqrt(jnp.sum(squares[...], axis=-1, keepdims=True) * (1.0 / 8192) + EPSILON)
+    cosine, sine = turn_ref[:, :HEAD], turn_ref[:, HEAD:]
+    for number in range(OWN_HEADS + 1):
+        columns = slice(HEAD * number, HEAD * number + HEAD)
+        head = total[:, columns] * scale + rows_ref[7:8, columns]
+        swapped = pltpu.roll(head, HEAD // 2, 1)
+        if number == OWN_HEADS:
+            turned = jnp.where(img == 0, head * cosine + swapped * sine, head)
+        else:
+            turned = head * cosine + swapped * sine
+        rows_out[:, columns] = turned.astype(jnp.bfloat16)
+
+
+def encode(count, start, patches, rows, turn, qkv, proj, merge_weight, text, part):
     vmem = pl.BlockSpec(memory_space=pltpu.VMEM)
     hbm = pl.BlockSpec(memory_space=pl.ANY)
     smem = pl.BlockSpec(memory_space=pltpu.SMEM)
     bf16, f32 = jnp.bfloat16, jnp.float32
     return pl.pallas_call(
         vision_kernel,
-        out_shape=(
-            jax.ShapeDtypeStruct((2, 256, 5 * HEAD), f32),
-            jax.ShapeDtypeStruct((256, 5 * HEAD), f32),
-        ),
-        in_specs=[smem] + [vmem] * 9 + [hbm] + [vmem] + [hbm] + [vmem] + [hbm],
-        out_specs=(vmem, vmem),
+        out_shape=jax.ShapeDtypeStruct((SECTION, 5 * HEAD), bf16),
+        in_specs=[smem] * 2 + [vmem] * 5 + [hbm] * 3,
+        out_specs=vmem,
         scratch_shapes=[
+            pltpu.VMEM((VW, 6 * HEAD), bf16),
             pltpu.VMEM((PATCH_CAP, 6 * HEAD), bf16),
+            pltpu.VMEM((2, HEAD, PATCH_CAP), bf16),
             pltpu.VMEM((PATCH_CAP, 2 * HEAD), bf16),
             pltpu.VMEM((8, 128, 2 * HEAD), bf16),
             pltpu.VMEM((8, 256, VW), bf16),
             pltpu.VMEM((4 * VW, 1024), bf16),
             pltpu.VMEM((VW // HEAD, 128, HEAD), f32),
             pltpu.VMEM((4, 256, VW), bf16),
-            pltpu.VMEM((8, 256, 1024), bf16),
             pltpu.VMEM((4, 4, 2, 256, 5 * HEAD), bf16),
-            pltpu.VMEM((4, 2, 256, 2048), bf16),
-            pltpu.VMEM((3, 256, HEAD), f32),
-            pltpu.SemaphoreType.DMA((53,)),
-            pltpu.SemaphoreType.DMA((53,)),
+            pltpu.VMEM((2, 256, 1024), bf16),
+            pltpu.VMEM((8, 4, SECTION, 256), bf16),
+            pltpu.VMEM((SECTION, 5 * HEAD), f32),
+            pltpu.VMEM((SECTION, HEAD), f32),
+            pltpu.SemaphoreType.DMA((98,)),
+            pltpu.SemaphoreType.DMA((98,)),
             pltpu.SemaphoreType.DMA((7,)),
             pltpu.SemaphoreType.DMA((8,)),
-            pltpu.SemaphoreType.DMA((3,)),
+            pltpu.SemaphoreType.DMA((4,)),
         ],
         compiler_params=pltpu.CompilerParams(
             collective_id=1, has_side_effects=True, vmem_limit_bytes=62 * 1024 * 1024
         ),
-    )(count, patches, gain, shift, qkv, qkv_bias, proj, proj_bias, merge_gain, merge_shift,
-      merge_weight, merge_bias, text, norm_gain, half)
+    )(count, start, patches, rows, turn, qkv, proj, merge_weight, text, part)
 
 
 def on_device(
@@ -653,41 +637,29 @@
     vision_proj, vision_proj_bias, merge_gain, merge_shift, merge_weight, merge_bias, text_embed,
     norm_gain, qkv_weight, qkv_bias,
 ):
-    count = patch_counts[0]
-    offset = image_offsets[0]
     img = lax.axis_index("img")
     wide_q = OWN_HEADS * HEAD
     f32 = jnp.float32
 
-    def halves(array):
-        first = jnp.concatenate([array[:, :wide_q], array[:, 2 * wide_q : 2 * wide_q + HEAD]], axis=1)
-        second = jnp.concatenate([array[:, wide_q : 2 * wide_q], array[:, 2 * wide_q + HEAD :]], axis=1)
-        return jnp.stack([first, second])
-
-    spare = ((0, 0), (0, 0), (0, HEAD - VHEAD))
-    wide_qkv = jnp.pad(vision_qkv.reshape(VW, 6, VHEAD), spare).reshape(VW, 6 * HEAD)
-    wide_bias = jnp.pad(vision_qkv_bias.astype(f32).reshape(1, 6, VHEAD), spare)
-    wide_bias = wide_bias.at[:, 2::3, VHEAD].set(1.0).reshape(1, 6 * HEAD)
-    from_text, from_vision = encode(
-        patch_counts, patches[0], vision_gain[None], vision_shift[None], wide_qkv, wide_bias,
-        vision_proj, vision_proj_bias[None], merge_gain[None], merge_shift[None], merge_weight,
-        merge_bias.astype(f32)[None], text_embed, norm_gain.astype(f32).reshape(8, 1, 1024),
-        halves(qkv_weight),
-    )
-    from_text = from_text.reshape(SECTION, 5 * HEAD)
-    bias = halves(qkv_bias[None])[img, 0]
-    my_start = lax.axis_index("seq") * SECTION
-    padded = jnp.pad(from_vision, ((SECTION, SECTION), (0, 0)))
-    where_at = jnp.clip(my_start - offset + SECTION, 0, PATCH_CAP // 4 + SECTION)
-    placed = lax.dynamic_slice_in_dim(padded, where_at, SECTION, 0)
-    positions = my_start + jnp.arange(SECTION, dtype=jnp.int32)
-    inside = (positions >= offset) & (positions < offset + count // 4)
-    projected = jnp.where(inside[:, None], placed, from_text) + bias.astype(f32)
-    heads = projected.reshape(SECTION, OWN_HEADS + 1, HEAD)
-    turned = rotary(heads, positions, HEAD)
-    last = jnp.where(img == 0, turned[:, OWN_HEADS:], heads[:, OWN_HEADS:])
-    rows = jnp.concatenate([turned[:, :OWN_HEADS], last], axis=1).astype(jnp.bfloat16)
-    return attend(rows.reshape(SECTION, (OWN_HEADS + 1) * HEAD))
+    def line(array):
+        return jnp.pad(array.astype(f32), (0, VW - array.shape[0]))[None]
+
+    first_bias = jnp.concatenate([qkv_bias[:wide_q], qkv_bias[2 * wide_q : 2 * wide_q + HEAD]])
+    second_bias = jnp.concatenate([qkv_bias[wide_q : 2 * wide_q], qkv_bias[2 * wide_q + HEAD :]])
+    own_bias = jnp.where(img == 0, first_bias, second_bias)
+    singles = [
+        vision_gain, vision_shift, vision_proj_bias, merge_gain, merge_shift, vision_qkv_bias, merge_bias, own_bias,
+    ]
+    gains = jnp.pad(norm_gain.astype(f32).reshape(8, 1024), ((0, 0), (0, VW - 1024)))
+    lines = jnp.concatenate([line(array) for array in singles] + [gains], axis=0)
+    positions = lax.axis_index("seq") * SECTION + jnp.arange(SECTION, dtype=jnp.int32)
+    cosine, sine = rotation(positions)
+    turn = jnp.concatenate([cosine, cosine, -sine, sine], axis=1)
+    rows = encode(
+        patch_counts, image_offsets, patches[0], lines, turn, vision_qkv, vision_proj, merge_weight, text_embed,
+        qkv_weight,
+    )
+    return attend(rows)
 
 
 def solution(mesh):

time: 205 us -> 190 us (0.927)
  Pallas kernels: 185 us -> 173 us
    pallas_call x1, Pallas kernels: 129 us -> 114 us  [encode(): pl.pallas_call(vision_kernel, out_shape=jax.ShapeDtypeStruct((SECTION, 5...]
    pallas_call x1, Pallas kernels: 56.7 us -> 59.1 us  [attend(): pl.pallas_call(attend_kernel, out_shape=jax.ShapeDtypeStruct((HALF, 2 * O...]
    broadcast_in_dim x6 -> x8, local copies, waits for them, and re-layouts: 4.38 us -> 3.53 us  [line(): return jnp.pad(array.astype(f32), (0, VW - array.shape[0]))[None]]
where the time goes in v4:
time: 190 us; the launch traced here: 188 us
  Pallas kernels  173 us (91%)
  local copies, waits for them, and re-layouts  10.4 us (5%)
  other arithmetic  3.46 us (2%)
    pallas_call x1, Pallas kernels, encode(): pl.pallas_call(vision_kernel, out_shape=jax.ShapeDtypeStruct((SECTION, 5...  114 us
    pallas_call x1, Pallas kernels, attend(): pl.pallas_call(attend_kernel, out_shape=jax.ShapeDtypeStruct((HALF, 2 * O...  59.1 us

profile of v4, /device:TPU:102, one launch (start us, length us, event | category | flops | bytes accessed | tf_op | source)
XLA Modules:
  0.0 188.1 jit_solution(4244494844266552074)
XLA Ops:
  0.0 0.0 copy-start.1
  1.4 0.8 fusion.2
  2.2 0.8 fusion.1
  3.0 0.7 broadcast_in_dim.35
  3.7 0.7 broadcast_in_dim.36
  4.4 0.7 broadcast_in_dim.37
  5.1 0.7 broadcast_in_dim.38
  5.8 0.7 broadcast_in_dim.39
  6.5 0.7 pad_convert_fusion.3
  7.2 0.7 pad_convert_fusion.2
  7.9 0.7 reshape.16
  8.6 1.3 concatenate.14.rows_ref
  9.9 1.0 multiply_cosine_fusion
  10.9 1.1 pad_maximum_fusion.turn_ref
  12.0 0.0 copy-done.1
  12.0 1.5 copy.20.qkv_ref
  13.4 113.6 %shard_map.163.x_ref = bf16[512,640]{1,0:T(8,128)(2,1)} custom-call(s32[1]{0:T(128)S(6)} %copy.22.count_ref, s32[1]{0:T(128)S(6)} %copy.23.start_ref, bf16[1024,1280]{1,0:T(8,128)(2,1)} %bitcast.1, f32[16,1280]{1,0:T(8,128)} %concatenate.14.rows_ref, f32[512,256]{1,0:T(8,128)} %pad_maximum_fusion.turn_ref, bf16[1280,480]{1,0:T(8,128)(2,1)} %copy.20.qkv_ref, ...), custom_call_target="tpu_custom_call" | custom-call | tf_op jit(solution)/shard_map/pallas_call | solution.py:603
  127.0 0.0 copy-start
  127.1 1.1 copy-done
  128.1 59.1 %shard_map.164 = bf16[256,1024]{1,0:T(8,128)(2,1)S(1)} custom-call(bf16[512,640]{1,0:T(8,128)(2,1)S(1)} %copy-done), custom_call_target="tpu_custom_call" | custom-call | tf_op jit(solution)/shard_map/pallas_call | solution.py:236
  187.3 0.8 copy.24
  (8 shorter events, 0.1 us)
Async XLA Ops:
  0.0 12.0 %copy-start.1 = (bf16[1280,480]{0,1:T(8,128)(2,1)S(1)}, bf16[1280,480]{0,1:T(8,128)(2,1)}, u32[]{:S(2)}) copy-start(bf16[1280,480]{0,1:T(8,128)(2,1)} %param.22) | copy-start | bytes 3686404
  127.0 1.1 copy-start

commit v5 on v4

v5 whole, which is shorter than its diff:
```python
import functools

import jax
import jax.numpy as jnp
from jax import lax
from jax.experimental import pallas as pl
from jax.experimental.pallas import tpu as pltpu
from jax.sharding import PartitionSpec as P

HEAD = 128
VW = 1280
PATCH_CAP = 1024
GROUP = 8
VHEAD = 80
SECTION = 512
HALF = 256
OWN_HEADS = 4

EPSILON = 1e-06
THETA = 1000000.0
MASKED = -1e30
LOG2E = 1.4426950408889634
MESH = pl.DeviceIdType.MESH


def rotation(positions):
    halfway = HEAD // 2
    frequency = jnp.power(jnp.float32(THETA), -(jnp.arange(halfway, dtype=jnp.float32) * 2.0) / HEAD)
    angles = positions.astype(jnp.float32)[:, None] * frequency[None, :]
    return jnp.cos(angles), jnp.sin(angles)


def grid_gather(copy, base, block, part, first, second, ahead, behind):
    before, after, far = (first + 3) % 4, (first + 1) % 4, (first + 2) % 4
    low, high = (second + 3) % 4, (second + 1) % 4

    def whole(number, a, way):
        return copy(block(a, second), block(a, second), base + number, way)

    def half(number, a, b, h, way):
        return copy(part(a, b, h), part(a, b, h), base + number, way)

    up, down = whole(0, first, ahead[0]), whole(1, first, behind[0])
    pass_up = half(2, before, second, 0, ahead[0])
    pass_down = half(3, after, second, 1, behind[0])
    columns = (first, before, after, far)
    over = [(whole(4 + 2 * n, a, ahead[1]), whole(5 + 2 * n, a, behind[1])) for n, a in enumerate(columns)]
    on = [
        (half(12 + 2 * n, a, low, 0, ahead[1]), half(13 + 2 * n, a, high, 1, behind[1]))
        for n, a in enumerate(columns)
    ]

    def spread(n):
        over[n][0].start()
        over[n][1].start()

    def relay(n):
        over[n][0].wait_recv()
        on[n][0].start()
        over[n][1].wait_recv()
        on[n][1].start()

    def begin():
        up.start()
        down.start()
        spread(0)

    def turn():
        up.wait_recv()
        pass_up.start()
        spread(1)
        down.wait_recv()
        pass_down.start()
        spread(2)

    def near():
        relay(0)

    def turned():
        pass_up.wait_recv()
        pass_down.wait_recv()
        spread(3)

    def middle():
        relay(1)
        relay(2)

    def last():
        relay(3)

    def done():
        for c in on:
            c[0].wait_recv()
            c[1].wait_recv()
        for c in [(up, down), (pass_up, pass_down)] + over + on:
            c[0].wait_send()
            c[1].wait_send()

    return begin, turn, near, turned, middle, last, done


def column_gather(copy, base, slot, part, y, core, device):
    before, after, far = (y + 3) % 4, (y + 1) % 4, (y + 2) % 4
    ahead, behind, sibling = device(after, core), device(before, core), device(y, 1 - core)
    own = slot(y, core)
    share = copy(own, own, base, sibling)
    send_up = copy(own, own, base + 1, ahead)
    send_down = copy(own, own, base + 2, behind)
    low, high = part(before, core, 0), part(after, core, 1)
    pass_up = copy(low, low, base + 3, ahead)
    pass_down = copy(high, high, base + 4, behind)
    left, right = slot(before, core), slot(after, core)
    give_left = copy(left, left, base + 5, sibling)
    give_right = copy(right, right, base + 6, sibling)
    far_low, far_high = part(far, core, 0), part(far, core, 1)
    give_low = copy(far_low, far_low, base + 7, sibling)
    give_high = copy(far_high, far_high, base + 8, sibling)

    def start():
        send_up.start()
        send_down.start()
        share.start()

    def turn():
        send_up.wait_recv()
        pass_up.start()
        give_left.start()
        send_down.wait_recv()
        pass_down.start()
        give_right.start()

    def last():
        pass_up.wait_recv()
        give_low.start()
        pass_down.wait_recv()
        give_high.start()

    def done():
        for c in (share, give_left, give_right, give_low, give_high):
            c.wait_recv()
        for c in (share, send_up, send_down, pass_up, pass_down, give_left, give_right, give_low, give_high):
            c.wait_send()

    return start, turn, last, done


def plane_spread(copy, base, give, slot, y, core, device):
    mate = y + 1 - 2 * (y % 2)
    straight = (y + 2) % 4
    across = straight + 1 - 2 * (straight % 2)
    own, sibling = slot(y, core), device(y, 1 - core)

    def send(src, number, peer):
        return copy(src, own, base + number, peer)

    share, near = send(own, 0, sibling), send(own, 1, device(mate, core))
    far, close = send(give, 2, device(straight, core)), send(give, 3, device(across, core))
    relays = [copy(slot(a, core), slot(a, core), base + 4 + n, sibling) for n, a in enumerate((mate, across, straight))]

    def start():
        near.start()
        close.start()
        far.start()
        share.start()

    def turn():
        for c, relay in zip((near, close, far), relays):
            c.wait_recv()
            relay.start()

    def done():
        for c in [share] + relays:
            c.wait_recv()
        for c in [share, near, far, close] + relays:
            c.wait_send()

    return start, turn, done


def vision_kernel(
    count_ref, start_ref, patches_ref, rows_ref, turn_ref, qkv_ref, proj_ref, merge_ref, text_ref, part_ref,
    out_ref,
    wide, mixed, flipped, ctx, ctx_in, proj_all, merge_w, lines, merge_in, weight, text_give, text, tok_give, tok,
    total, squares, sums, part_out, part_in, buf, guest, top, acc,
    send, recv, ctx_send, ctx_recv, local,
):
    seq = lax.axis_index("seq")
    tp = lax.axis_index("tp")
    img = lax.axis_index("img")
    x, z = seq // 4, seq % 4
    core, y = tp % 2, img * 2 + tp // 2
    me = tp * 2 + img
    gain, shift, proj_bias, merge_gain, merge_shift = [rows_ref[n : n + 1, :] for n in range(5)]

    def device(y_at, core_at):
        return {"tp": 2 * (y_at % 2) + core_at, "img": y_at // 2}

    def order(y_at, core_at):
        return (2 * (y_at % 2) + core_at) * 2 + y_at // 2

    def along_x(d):
        return {"seq": ((x + d) % 4) * 4 + z}

    def along_z(d):
        return {"seq": x * 4 + (z + d) % 4}

    def member(index):
        return {"tp": index // 2, "img": index % 2}

    peers = [member((me + d) % 8) for d in range(1, 8)]
    mirror = 15 - seq
    peers += [along_x(1), along_x(3), along_z(1), along_z(3), {"seq": mirror}, {"seq": mirror, "img": 1 - img}]
    barrier = pltpu.get_barrier_semaphore()
    for peer in peers:
        pl.semaphore_signal(barrier, inc=1, device_id=peer, device_id_type=MESH)
    load_merge = pltpu.make_async_copy(merge_ref, merge_w, local.at[0])
    load_merge.start()
    load_weight = pltpu.make_async_copy(part_ref, weight.at[x, z], local.at[1])
    load_weight.start()
    load_text = []
    for n in range(4):
        columns = pl.ds(256 * n, 256)
        for parity, target in ((1 - img, text_give.at[:, columns]), (img, text.at[tp, img, :, columns])):
            at = pl.ds(pl.multiple_of((2 * n + parity) * 256, 256), 256)
            load_text.append(pltpu.make_async_copy(text_ref.at[:, at], target, local.at[2 + len(load_text)]))
    for c in load_text:
        c.start()
    proj_all[:, 2 * VHEAD :, :] = jnp.zeros((8, 256 - 2 * VHEAD, VW), jnp.bfloat16)
    proj_all[me, : 2 * VHEAD, :] = proj_ref[...]
    pl.semaphore_wait(barrier, len(peers))

    def remote(src, dst, out, into, peer):
        return pltpu.make_async_remote_copy(
            src_ref=src,
            dst_ref=dst,
            send_sem=send.at[out],
            recv_sem=recv.at[into],
            device_id=peer,
            device_id_type=MESH,
        )

    def copy(src, dst, number, peer):
        return remote(src, dst, number, number, peer)

    proj_gather = column_gather(
        copy, 0,
        lambda a, b: proj_all.at[order(a, b), pl.ds(0, 160)],
        lambda a, b, h: proj_all.at[order(a, b), pl.ds(80 * h, 80)],
        y, core, device,
    )
    merge_gather = column_gather(
        copy, 9,
        lambda a, b: merge_in.at[:, pl.ds(order(a, b) * 32, 32)],
        lambda a, b, h: merge_in.at[pl.ds(2 * h, 2), pl.ds(order(a, b) * 32, 32)],
        y, core, device,
    )
    text_spread = [
        plane_spread(
            copy, 18 + 7 * n, text_give.at[pl.ds(128 * n, 128)],
            lambda a, b, n=n: text.at[2 * (a % 2) + b, a // 2, pl.ds(128 * n, 128)],
            y, core, device,
        )
        for n in range(2)
    ]
    token_spread = [
        plane_spread(copy, 32 + 7 * n, tok_give.at[n], lambda a, b, n=n: tok.at[order(a, b), n], y, core, device)
        for n in range(2)
    ]
    other = {"img": 1 - img}
    quarter, fifth = pl.ds(0, 4 * HEAD), pl.ds(4 * HEAD, HEAD)
    trade = [
        copy(sums.at[0], sums.at[1], 47, other),
        copy(part_out.at[:, fifth], part_in.at[:, fifth], 46, other),
        copy(part_out.at[:, quarter], part_in.at[:, quarter], 133, other),
    ]
    two = 2 * HEAD
    query = merge_w.at[pl.ds(0, 4 * SECTION), pl.ds(0, HEAD)]
    lent = merge_w.at[pl.ds(0, SECTION), pl.ds(HEAD, two)]
    away = merge_w.at[pl.ds(0, SECTION), pl.ds(HEAD + two, two)]
    home = merge_w.at[pl.ds(0, SECTION), pl.ds(HEAD + 2 * two, two)]
    ways = (along_x(1), along_z(1)), (along_x(3), along_z(3))
    weight_one = grid_gather(
        copy, 48,
        lambda a, b: weight.at[a, b, pl.ds(0, 128)],
        lambda a, b, h: weight.at[a, b, pl.ds(64 * h, 64)],
        x, z, ways[0], ways[1],
    )
    weight_two = grid_gather(
        copy, 68,
        lambda a, b: weight.at[b, a, pl.ds(128, 128)],
        lambda a, b, h: weight.at[b, a, pl.ds(128 + 64 * h, 64)],
        z, x, ways[0][::-1], ways[1][::-1],
    )

    proj_gather[0]()
    load_weight.wait()
    weight_one[0]()
    weight_two[0]()

    def norm(source, scaling, shifting):
        average = jnp.mean(source, axis=-1, keepdims=True)
        centred = source - average
        spread = jnp.mean(centred * centred, axis=-1, keepdims=True)
        return centred * lax.rsqrt(spread + EPSILON) * scaling + shifting

    old = lax.broadcasted_iota(jnp.int32, (6 * VHEAD, 6 * HEAD), 0)
    new = lax.broadcasted_iota(jnp.int32, (6 * VHEAD, 6 * HEAD), 1)
    place = ((old // VHEAD == new // HEAD) & (old % VHEAD == new % HEAD)).astype(jnp.float32).astype(jnp.bfloat16)
    wide[...] = jnp.dot(qkv_ref[...], place, preferred_element_type=jnp.float32).astype(jnp.bfloat16)
    bias = jnp.dot(
        rows_ref[5:6, : 6 * VHEAD].astype(jnp.bfloat16), place, preferred_element_type=jnp.float32
    )
    column = lax.broadcasted_iota(jnp.int32, (1, 6 * HEAD), 1)
    bias = bias + ((column % HEAD == VHEAD) & ((column // HEAD) % 3 == 2)).astype(jnp.float32)

    def mix(number, carry):
        rows = pl.ds(pl.multiple_of(number * 512, 512), 512)
        normed = norm(patches_ref[rows, :].astype(jnp.float32), gain, shift)
        product = jnp.dot(normed.astype(jnp.bfloat16), wide[...], preferred_element_type=jnp.float32) + bias
        mixed[rows, :] = product.astype(jnp.bfloat16)
        for head in range(2):
            keys = product[:, 384 * head + 128 : 384 * head + 256].T
            flipped[head, :, rows] = keys.astype(jnp.bfloat16)
        return carry

    lax.fori_loop(0, 2, mix, 0)
    for c in load_text:
        c.wait()
    valid = lax.broadcasted_iota(jnp.int32, (512, PATCH_CAP), 1) < count_ref[0]
    lane = lax.broadcasted_iota(jnp.int32, (512, HEAD), 1)

    def look(number):
        rows = pl.ds(pl.multiple_of(number * 512, 512), 512)
        parts = []
        for head in range(2):
            query = mixed[rows, 384 * head : 384 * head + 128]
            values = mixed[:, 384 * head + 256 : 384 * head + 384]
            scores = jnp.dot(query, flipped[head], preferred_element_type=jnp.float32)
            scores = jnp.where(valid, scores * (VHEAD ** (-0.5) * LOG2E), MASKED)
            best = jnp.max(scores, axis=-1, keepdims=True) + jnp.zeros((512, HEAD), jnp.float32)
            weights = [jnp.exp2(scores[:, n * HEAD : (n + 1) * HEAD] - best) for n in range(8)]
            weights = jnp.concatenate(weights, axis=1).astype(jnp.bfloat16)
            product = jnp.dot(weights, values, preferred_element_type=jnp.float32)
            parts.append(product / product[:, VHEAD : VHEAD + 1])
        turned = pltpu.roll(parts[1], VHEAD, 1)
        ctx[rows, :HEAD] = jnp.where(lane < VHEAD, parts[0], turned).astype(jnp.bfloat16)
        ctx[rows, HEAD:] = jnp.where(lane < 2 * VHEAD - HEAD, turned, 0.0).astype(jnp.bfloat16)

    def ctx_copy(number, target):
        return pltpu.make_async_remote_copy(
            src_ref=ctx.at[pl.ds(pl.multiple_of(target * 128, 128), 128)],
            dst_ref=ctx_in.at[me],
            send_sem=ctx_send.at[number],
            recv_sem=ctx_recv.at[me],
            device_id=member(target),
            device_id_type=MESH,
        )

    side = me // 4
    look(1 - side)
    for n in range(4):
        ctx_copy(n, (1 - side) * 4 + n).start()
    proj_gather[1]()
    look(side)
    for n in range(3):
        ctx_copy(4 + n, side * 4 + (me + 1 + n) % 4).start()
    ctx_in[me] = ctx[pl.ds(pl.multiple_of(me * 128, 128), 128), :]
    proj_gather[2]()
    weight_one[1]()
    weight_two[1]()
    weight_one[2]()
    weight_two[2]()

    def arrived(number, carry):
        source = (me + 1 + number) % 8
        pltpu.make_async_remote_copy(
            src_ref=ctx.at[pl.ds(0, 128)],
            dst_ref=ctx_in.at[source],
            send_sem=ctx_send.at[number],
            recv_sem=ctx_recv.at[source],
            device_id=member(source),
            device_id_type=MESH,
        ).wait()
        return carry

    lax.fori_loop(0, 7, arrived, 0)
    text_spread[0][0]()
    proj_gather[3]()
    weight_one[3]()
    weight_two[3]()
    resid = patches_ref[pl.ds(me * 128, 128), :].astype(jnp.float32) + proj_bias
    for number in range(8):
        resid = resid + jnp.dot(ctx_in[number], proj_all[number], preferred_element_type=jnp.float32)
    settled = norm(resid, merge_gain, merge_shift)
    for tile in range(VW // HEAD):
        lines[tile] = settled[:, tile * HEAD : (tile + 1) * HEAD]
    for number in range(4):
        picked = [lines[tile, pl.ds(number, 32, stride=4), :] for tile in range(VW // HEAD)]
        merge_in[number, pl.ds(me * 32, 32), :] = jnp.concatenate(picked, axis=1).astype(jnp.bfloat16)
    merge_gather[0]()
    load_merge.wait()
    merge_gather[1]()
    weight_one[4]()
    weight_two[4]()
    merge_gather[2]()
    text_spread[0][1]()
    text_spread[1][0]()
    first = start_ref[0] - seq * SECTION
    spot = lax.broadcasted_iota(jnp.int32, (SECTION, 256), 0) - first
    slot = lax.broadcasted_iota(jnp.int32, (SECTION, 256), 1)
    pick = ((spot == slot) & (slot < count_ref[0] // 4)).astype(jnp.float32).astype(jnp.bfloat16)
    merge_gather[3]()
    spot = lax.broadcasted_iota(jnp.int32, (SECTION, 512), 0) - first
    inside = (spot >= 0) & (spot < count_ref[0] // 4)

    def merge(number):
        columns = pl.ds(pl.multiple_of(number * 256, 256), 256)
        token = rows_ref[6:7, columns]
        for part in range(4):
            token = token + jnp.dot(
                merge_in[part], merge_w[pl.ds(part * VW, VW), columns], preferred_element_type=jnp.float32
            )
        return token.astype(jnp.bfloat16)

    for n in range(2):
        tok_give[n] = merge(2 * n + 1 - img)
        tok[me, n] = merge(2 * n + img)
        token_spread[n][0]()
    squares[...] = jnp.zeros_like(squares)
    total[...] = jnp.zeros_like(total)
    weight_one[5]()
    weight_two[5]()

    def weigh(chunk):
        token = jnp.concatenate([tok[chunk, 0], tok[chunk, 1]], axis=1)
        placed = jnp.dot(pick, token, preferred_element_type=jnp.float32)
        words = text[chunk // 2, :, :, pl.ds(pl.multiple_of((chunk % 2) * 512, 512), 512)]
        values = jnp.where(inside, placed, words.reshape(SECTION, 512).astype(jnp.float32))
        gains = [rows_ref[pl.ds(8 + chunk, 1), pl.ds(pl.multiple_of(512 * n + img * 256, 256), 256)] for n in range(2)]
        scaled = (values * jnp.concatenate(gains, axis=1)).astype(jnp.bfloat16)
        folded = jnp.zeros((SECTION, HEAD), jnp.float32)
        for number in range(4):
            piece = values[:, number * HEAD : (number + 1) * HEAD]
            folded = folded + piece * piece
        w = weight[chunk // 2, pl.ds((chunk % 2) * 2, 2)].reshape(512, 10 * HEAD)
        total[...] += jnp.dot(scaled, w, preferred_element_type=jnp.float32)
        squares[...] += folded

    text_spread[0][2]()
    text_spread[1][1]()
    token_spread[0][1]()
    token_spread[1][1]()
    text_spread[1][2]()
    weight_one[6]()
    weight_two[6]()

    def ours(number, carry):
        weigh(order((y + number) % 4, core))
        return carry

    def theirs(number, carry):
        weigh(order((y + number) % 4, 1 - core))
        return carry

    lax.fori_loop(0, 4, ours, 0)
    token_spread[0][2]()
    token_spread[1][2]()
    lax.fori_loop(0, 4, theirs, 0)

    def taken(side, size, start):
        return total[:, pl.ds(pl.multiple_of(start + side * size, HEAD), size)]

    part_out[:, : 4 * HEAD] = taken(1 - img, 4 * HEAD, 0).astype(jnp.bfloat16)
    part_out[:, 4 * HEAD :] = taken(1 - img, HEAD, 8 * HEAD).astype(jnp.bfloat16)
    sums[0] = jnp.sum(squares[...].T, axis=0, keepdims=True) + jnp.zeros((8, SECTION), jnp.float32)
    for c in trade:
        c.start()
    gather_one = grid_gather(
        copy, 90,
        lambda a, b: buf.at[img, a, b],
        lambda a, b, h: buf.at[img, a, b, pl.ds(HALF * h, HALF)],
        x, z, ways[0], ways[1],
    )
    gather_two = grid_gather(
        copy, 110,
        lambda a, b: buf.at[1 - img, b, a],
        lambda a, b, h: buf.at[1 - img, b, a, pl.ds(HALF * h, HALF)],
        z, x, ways[0][::-1], ways[1][::-1],
    )
    top[...] = jnp.full_like(top, MASKED)
    acc[...] = jnp.zeros_like(acc)
    trade[0].wait()
    mean = (sums[0, 0:1] + sums[1, 0:1]) * (1.0 / 8192)
    scale = (lax.rsqrt(mean + EPSILON) + jnp.zeros((HEAD, SECTION), jnp.float32)).T
    cosine, sine = turn_ref[:, :HEAD], turn_ref[:, HEAD:]

    def settle(mine, number):
        columns = slice(HEAD * number, HEAD * number + HEAD)
        head = (mine + part_in[:, columns].astype(jnp.float32)) * scale + rows_ref[7:8, columns]
        return head, head * cosine + pltpu.roll(head, HEAD // 2, 1) * sine

    trade[1].wait()
    plain, turned = settle(taken(img, HEAD, 8 * HEAD), OWN_HEADS)
    columns = [turned[n * HEAD : (n + 1) * HEAD].T for n in range(SECTION // HEAD)]
    buf[img, x, z] = jnp.where(img == 0, jnp.concatenate(columns, axis=0), plain).astype(jnp.bfloat16)
    swap = copy(buf.at[img, x, z], buf.at[img, x, z], 88, other)
    swap.start()
    gather_one[0]()
    trade[2].wait()
    heads = [settle(taken(img, 4 * HEAD, 0)[:, n * HEAD : n * HEAD + HEAD], n)[1].astype(jnp.bfloat16) for n in range(4)]
    for n in range(2):
        lent[:, n * HEAD : n * HEAD + HEAD] = heads[2 + n]
        query[pl.ds(n * SECTION, SECTION), :] = heads[n]
    lend = copy(lent, guest, 89, {"seq": mirror})
    lend.start()
    rows_all = 2 * SECTION
    ones = jnp.ones((SECTION, HEAD), jnp.bfloat16)
    tiles = SECTION // HEAD

    def block(group, number, masked):
        rows = pl.ds(pl.multiple_of(group * rows_all, rows_all), rows_all)
        a, b = number // 4, number % 4
        keys = jnp.concatenate([buf[0, a, b, n * HEAD : (n + 1) * HEAD] for n in range(tiles)], axis=1)
        values = jnp.concatenate([buf[1, a, b], ones], axis=1)
        scores = jnp.dot(query[rows, :], keys, preferred_element_type=jnp.float32)
        scores = scores * (HEAD ** (-0.5) * LOG2E)
        if masked:
            row = lax.broadcasted_iota(jnp.int32, (rows_all, SECTION), 0) % SECTION
            col = lax.broadcasted_iota(jnp.int32, (rows_all, SECTION), 1)
            scores = jnp.where(col <= row, scores, MASKED)
        old = top[rows, :]
        new = jnp.maximum(old, jnp.max(scores, axis=-1, keepdims=True))
        factor = jnp.exp2(old - new)
        weights = [jnp.exp2(scores[:, n * HEAD : (n + 1) * HEAD] - new) for n in range(tiles)]
        weights = jnp.concatenate(weights, axis=1).astype(jnp.bfloat16)
        product = jnp.dot(weights, values, preferred_element_type=jnp.float32)
        top[rows, :] = new
        acc[rows, :] = acc[rows, :] * jnp.concatenate([factor, factor], axis=1) + product

    def visit(group, dx, dz):
        number = ((x + dx) % 4) * 4 + (z + dz) % 4

        @pl.when(number < group * mirror + (1 - group) * seq)
        def _():
            block(group, number, False)

    def both(count, offset):
        def step(n, carry):
            visit(n % 2, *offset(n // 2))
            return carry

        lax.fori_loop(0, 2 * count, step, 0)

    def ending(group):
        def across(n, carry):
            visit(group, 2, n)
            return carry

        def along(n, carry):
            visit(group, n * (n + 1) // 2, 2)
            return carry

        lax.fori_loop(0, 4, across, 0)
        lax.fori_loop(0, 3, along, 0)

    def finish(group):
        parts = []
        for head in range(2):
            total = acc[pl.ds(group * rows_all + head * SECTION, SECTION), :]
            parts.append((total[:, :HEAD] / total[:, HEAD:]).astype(jnp.bfloat16))
        return jnp.concatenate(parts, axis=1)

    swap.wait()
    gather_two[0]()
    block(0, seq, True)
    gather_one[1]()
    gather_two[1]()
    gather_one[2]()
    gather_two[2]()
    lend.wait()
    for head in range(2):
        query[pl.ds(rows_all + head * SECTION, SECTION), :] = guest[:, head * HEAD : (head + 1) * HEAD]
    visit(1, 0, 0)
    both(2, lambda n: (1 + 2 * n, 0))
    gather_one[3]()
    gather_two[3]()
    both(2, lambda n: (0, 1 + 2 * n))
    gather_one[4]()
    gather_two[4]()
    block(1, mirror, True)
    gather_one[5]()
    gather_two[5]()
    both(4, lambda n: (1 + 2 * (n // 2), 1 + 2 * (n % 2)))
    gather_one[6]()
    gather_two[6]()
    ending(1)
    away[...] = finish(1)
    to_mirror = [
        remote(
            away.at[pl.ds(HALF * n, HALF)],
            out_ref.at[:, pl.ds(pl.multiple_of(img * 2 * two + two, two), two)],
            130 + n, 130 + img, {"seq": mirror, "img": n},
        )
        for n in range(2)
    ]
    for c in to_mirror:
        c.start()
    ending(0)
    home[...] = finish(0)
    columns = pl.ds(pl.multiple_of(img * 2 * two, two), two)
    back = copy(home.at[pl.ds(pl.multiple_of((1 - img) * HALF, HALF), HALF)], out_ref.at[:, columns], 132, other)
    back.start()
    out_ref[:, columns] = home[pl.ds(pl.multiple_of(img * HALF, HALF), HALF), :]
    for n in range(2):
        to_mirror[n].wait_send()
        remote(
            away.at[pl.ds(HALF * n, HALF)],
            out_ref.at[:, pl.ds(n * 2 * two + two, two)],
            130 + n, 130 + n, {"seq": mirror, "img": n},
        ).wait_recv()
    back.wait()


def encode(count, start, patches, rows, turn, qkv, proj, merge_weight, text, part):
    vmem = pl.BlockSpec(memory_space=pltpu.VMEM)
    hbm = pl.BlockSpec(memory_space=pl.ANY)
    smem = pl.BlockSpec(memory_space=pltpu.SMEM)
    bf16, f32 = jnp.bfloat16, jnp.float32
    return pl.pallas_call(
        vision_kernel,
        out_shape=jax.ShapeDtypeStruct((HALF, 2 * OWN_HEADS * HEAD), bf16),
        in_specs=[smem] * 2 + [vmem] * 5 + [hbm] * 3,
        out_specs=vmem,
        scratch_shapes=[
            pltpu.VMEM((VW, 6 * HEAD), bf16),
            pltpu.VMEM((PATCH_CAP, 6 * HEAD), bf16),
            pltpu.VMEM((2, HEAD, PATCH_CAP), bf16),
            pltpu.VMEM((PATCH_CAP, 2 * HEAD), bf16),
            pltpu.VMEM((8, 128, 2 * HEAD), bf16),
            pltpu.VMEM((8, 256, VW), bf16),
            pltpu.VMEM((4 * VW, 1024), bf16),
            pltpu.VMEM((VW // HEAD, 128, HEAD), f32),
            pltpu.VMEM((4, 256, VW), bf16),
            pltpu.VMEM((4, 4, 256, 10 * HEAD), bf16),
            pltpu.VMEM((256, 1024), bf16),
            pltpu.VMEM((4, 2, 256, 1024), bf16),
            pltpu.VMEM((2, 256, 256), bf16),
            pltpu.VMEM((8, 2, 256, 256), bf16),
            pltpu.VMEM((SECTION, 10 * HEAD), f32),
            pltpu.VMEM((SECTION, HEAD), f32),
            pltpu.VMEM((2, 8, SECTION), f32),
            pltpu.VMEM((SECTION, 5 * HEAD), bf16),
            pltpu.VMEM((SECTION, 5 * HEAD), bf16),
            pltpu.VMEM((2, 4, 4, SECTION, HEAD), bf16),
            pltpu.VMEM((SECTION, 2 * HEAD), bf16),
            pltpu.VMEM((4 * SECTION, HEAD), f32),
            pltpu.VMEM((4 * SECTION, 2 * HEAD), f32),
            pltpu.SemaphoreType.DMA((134,)),
            pltpu.SemaphoreType.DMA((134,)),
            pltpu.SemaphoreType.DMA((7,)),
            pltpu.SemaphoreType.DMA((8,)),
            pltpu.SemaphoreType.DMA((10,)),
        ],
        compiler_params=pltpu.CompilerParams(
            collective_id=1, has_side_effects=True, vmem_limit_bytes=62 * 1024 * 1024
        ),
    )(count, start, patches, rows, turn, qkv, proj, merge_weight, text, part)


def on_device(
    patches, patch_counts, image_offsets, vision_gain, vision_shift, vision_qkv, vision_qkv_bias,
    vision_proj, vision_proj_bias, merge_gain, merge_shift, merge_weight, merge_bias, text_embed,
    norm_gain, qkv_weight, qkv_bias,
):
    img = lax.axis_index("img")
    wide_q = OWN_HEADS * HEAD
    f32 = jnp.float32

    def line(array):
        return jnp.pad(array.astype(f32), (0, VW - array.shape[0]))[None]

    first_bias = jnp.concatenate([qkv_bias[:wide_q], qkv_bias[2 * wide_q : 2 * wide_q + HEAD]])
    second_bias = jnp.concatenate([qkv_bias[wide_q : 2 * wide_q], qkv_bias[2 * wide_q + HEAD :]])
    own_bias = jnp.where(img == 0, first_bias, second_bias)
    singles = [
        vision_gain, vision_shift, vision_proj_bias, merge_gain, merge_shift, vision_qkv_bias, merge_bias, own_bias,
    ]
    gains = jnp.pad(norm_gain.astype(f32).reshape(8, 1024), ((0, 0), (0, VW - 1024)))
    lines = jnp.concatenate([line(array) for array in singles] + [gains], axis=0)
    positions = lax.axis_index("seq") * SECTION + jnp.arange(SECTION, dtype=jnp.int32)
    cosine, sine = rotation(positions)
    turn = jnp.concatenate([cosine, cosine, -sine, sine], axis=1)
    return encode(
        patch_counts, image_offsets, patches[0], lines, turn, vision_qkv, vision_proj, merge_weight, text_embed,
        qkv_weight,
    )


def solution(mesh):
    placed = (
        P("seq", None, None),
        P("seq"),
        P("seq"),
        P(),
        P(),
        P(None, ("tp", "img")),
        P(("tp", "img")),
        P(("tp", "img"), None),
        P(),
        P(),
        P(),
        P(None, ("tp", "img")),
        P(("tp", "img")),
        P(("seq", "img"), "tp"),
        P(),
        P(("seq", "img"), "tp"),
        P("tp"),
    )
    return jax.shard_map(
        on_device, mesh=mesh, in_specs=placed, out_specs=P(("seq", "img"), "tp"), check_vma=False
    )
```

time: 190 us -> 171 us (0.900)
  Pallas kernels: 173 us -> 153 us
    pallas_call x2 -> x1, Pallas kernels: 173 us -> 153 us  [encode(): pl.pallas_call(vision_kernel, out_shape=jax.ShapeDtypeStruct((HALF, 2 * O...]
where the time goes in v5:
time: 171 us; the launch traced here: 168 us
  Pallas kernels  153 us (89%)
  local copies, waits for them, and re-layouts  10.4 us (6%)
  other arithmetic  3.46 us (2%)
    pallas_call x1, Pallas kernels, encode(): pl.pallas_call(vision_kernel, out_shape=jax.ShapeDtypeStruct((HALF, 2 * O...  153 us
    broadcast_in_dim x8, local copies, waits for them, and re-layouts, line(): return jnp.pad(array.astype(f32), (0, VW - array.shape[0]))[None]  3.53 us

profile of v5, /device:TPU:102, one launch (start us, length us, event | category | flops | bytes accessed | tf_op | source)
XLA Modules:
  0.0 168.3 jit_solution(2392786209941059889)
XLA Ops:
  0.0 0.0 copy-start
  1.4 0.8 fusion.2
  2.2 0.8 fusion.1
  3.0 0.7 broadcast_in_dim.35
  3.7 0.7 broadcast_in_dim.36
  4.4 0.7 broadcast_in_dim.37
  5.1 0.7 broadcast_in_dim.38
  5.8 0.7 broadcast_in_dim.39
  6.5 0.7 pad_convert_fusion.3
  7.2 0.7 pad_convert_fusion.2
  7.9 0.7 reshape.16
  8.6 1.3 concatenate.14.rows_ref
  9.9 1.0 multiply_cosine_fusion
  10.9 1.1 pad_maximum_fusion.turn_ref
  12.0 0.0 copy-done
  12.0 1.5 copy.20.qkv_ref
  13.4 153.0 %shard_map.163 = bf16[256,1024]{1,0:T(8,128)(2,1)} custom-call(s32[1]{0:T(128)S(6)} %copy.22.count_ref, s32[1]{0:T(128)S(6)} %copy.23.start_ref, bf16[1024,1280]{1,0:T(8,128)(2,1)} %bitcast.1, f32[16,1280]{1,0:T(8,128)} %concatenate.14.rows_ref, f32[512,256]{1,0:T(8,128)} %pad_maximum_fusion.turn_ref, bf16[1280,480]{1,0:T(8,128)(2,1)} %copy.20.qkv_ref, ...), custom_call_target="tpu_custom_call" | custom-call | tf_op jit(solution)/shard_map/pallas_call | solution.py:629
  166.5 1.9 %copy.24 = bf16[256,1024]{1,0:T(8,128)(2,1)} copy(bf16[256,1024]{1,0:T(8,128)(2,1)} %shard_map.163) | data formatting | bytes 1048576
  (8 shorter events, 0.1 us)
Async XLA Ops:
  0.0 12.0 %copy-start = (bf16[1280,480]{0,1:T(8,128)(2,1)S(1)}, bf16[1280,480]{0,1:T(8,128)(2,1)}, u32[]{:S(2)}) copy-start(bf16[1280,480]{0,1:T(8,128)(2,1)} %param.22) | copy-start | bytes 3686404

commit v6 on v5

--- a/solution.py
+++ b/solution.py
@@ -178,9 +178,10 @@
 
 
 def vision_kernel(
-    count_ref, start_ref, patches_ref, rows_ref, turn_ref, qkv_ref, proj_ref, merge_ref, text_ref, part_ref,
-    out_ref,
-    wide, mixed, flipped, ctx, ctx_in, proj_all, merge_w, lines, merge_in, weight, text_give, text, tok_give, tok,
+    count_ref, start_ref, patches_ref, gain_ref, shift_ref, proj_bias_ref, merge_gain_ref, merge_shift_ref,
+    qkv_bias_ref, merge_bias_ref, norm_ref, bias_ref, cos_ref, sin_ref, qkv_ref, proj_ref, merge_ref, text_ref,
+    part_ref, out_ref,
+    rows_ref, wide, mixed, flipped, ctx, ctx_in, proj_all, merge_w, lines, merge_in, weight, text_give, text, tok_give, tok,
     total, squares, sums, part_out, part_in, buf, guest, top, acc,
     send, recv, ctx_send, ctx_recv, local,
 ):
@@ -190,6 +191,16 @@
     x, z = seq // 4, seq % 4
     core, y = tp % 2, img * 2 + tp // 2
     me = tp * 2 + img
+    singles = (gain_ref, shift_ref, proj_bias_ref, merge_gain_ref, merge_shift_ref, qkv_bias_ref, merge_bias_ref)
+    for n, ref in enumerate(singles):
+        rows_ref[n : n + 1, : ref.shape[0]] = ref[...].astype(jnp.float32)[None, :]
+    bias_row = bias_ref[...].astype(jnp.float32)[None, :]
+    q_bias = jnp.where(img == 0, bias_row[:, : 4 * HEAD], bias_row[:, 4 * HEAD : 8 * HEAD])
+    kv_bias = jnp.where(img == 0, bias_row[:, 8 * HEAD : 9 * HEAD], bias_row[:, 9 * HEAD :])
+    rows_ref[7:8, : 5 * HEAD] = jnp.concatenate([q_bias, kv_bias], axis=1)
+    norm_row = norm_ref[...].astype(jnp.float32)[None, :]
+    for n in range(8):
+        rows_ref[8 + n : 9 + n, :1024] = norm_row[:, n * 1024 : (n + 1) * 1024]
     gain, shift, proj_bias, merge_gain, merge_shift = [rows_ref[n : n + 1, :] for n in range(5)]
 
     def device(y_at, core_at):
@@ -306,7 +317,9 @@
     old = lax.broadcasted_iota(jnp.int32, (6 * VHEAD, 6 * HEAD), 0)
     new = lax.broadcasted_iota(jnp.int32, (6 * VHEAD, 6 * HEAD), 1)
     place = ((old // VHEAD == new // HEAD) & (old % VHEAD == new % HEAD)).astype(jnp.float32).astype(jnp.bfloat16)
-    wide[...] = jnp.dot(qkv_ref[...], place, preferred_element_type=jnp.float32).astype(jnp.bfloat16)
+    wide[...] = lax.dot_general(
+        qkv_ref[...], place, (((0,), (0,)), ((), ())), preferred_element_type=jnp.float32
+    ).astype(jnp.bfloat16)
     bias = jnp.dot(
         rows_ref[5:6, : 6 * VHEAD].astype(jnp.bfloat16), place, preferred_element_type=jnp.float32
     )
@@ -492,7 +505,8 @@
     trade[0].wait()
     mean = (sums[0, 0:1] + sums[1, 0:1]) * (1.0 / 8192)
     scale = (lax.rsqrt(mean + EPSILON) + jnp.zeros((HEAD, SECTION), jnp.float32)).T
-    cosine, sine = turn_ref[:, :HEAD], turn_ref[:, HEAD:]
+    cosine = jnp.concatenate([cos_ref[...], cos_ref[...]], axis=1)
+    sine = jnp.concatenate([-sin_ref[...], sin_ref[...]], axis=1)
 
     def settle(mine, number):
         columns = slice(HEAD * number, HEAD * number + HEAD)
@@ -621,7 +635,7 @@
     back.wait()
 
 
-def encode(count, start, patches, rows, turn, qkv, proj, merge_weight, text, part):
+def encode(*operands):
     vmem = pl.BlockSpec(memory_space=pltpu.VMEM)
     hbm = pl.BlockSpec(memory_space=pl.ANY)
     smem = pl.BlockSpec(memory_space=pltpu.SMEM)
@@ -629,9 +643,10 @@
     return pl.pallas_call(
         vision_kernel,
         out_shape=jax.ShapeDtypeStruct((HALF, 2 * OWN_HEADS * HEAD), bf16),
-        in_specs=[smem] * 2 + [vmem] * 5 + [hbm] * 3,
+        in_specs=[smem] * 2 + [vmem] * 14 + [hbm] * 3,
         out_specs=vmem,
         scratch_shapes=[
+            pltpu.VMEM((16, VW), f32),
             pltpu.VMEM((VW, 6 * HEAD), bf16),
             pltpu.VMEM((PATCH_CAP, 6 * HEAD), bf16),
             pltpu.VMEM((2, HEAD, PATCH_CAP), bf16),
@@ -664,7 +679,7 @@
         compiler_params=pltpu.CompilerParams(
             collective_id=1, has_side_effects=True, vmem_limit_bytes=62 * 1024 * 1024
         ),
-    )(count, start, patches, rows, turn, qkv, proj, merge_weight, text, part)
+    )(*operands)
 
 
 def on_device(
@@ -672,27 +687,12 @@
     vision_proj, vision_proj_bias, merge_gain, merge_shift, merge_weight, merge_bias, text_embed,
     norm_gain, qkv_weight, qkv_bias,
 ):
-    img = lax.axis_index("img")
-    wide_q = OWN_HEADS * HEAD
-    f32 = jnp.float32
-
-    def line(array):
-        return jnp.pad(array.astype(f32), (0, VW - array.shape[0]))[None]
-
-    first_bias = jnp.concatenate([qkv_bias[:wide_q], qkv_bias[2 * wide_q : 2 * wide_q + HEAD]])
-    second_bias = jnp.concatenate([qkv_bias[wide_q : 2 * wide_q], qkv_bias[2 * wide_q + HEAD :]])
-    own_bias = jnp.where(img == 0, first_bias, second_bias)
-    singles = [
-        vision_gain, vision_shift, vision_proj_bias, merge_gain, merge_shift, vision_qkv_bias, merge_bias, own_bias,
-    ]
-    gains = jnp.pad(norm_gain.astype(f32).reshape(8, 1024), ((0, 0), (0, VW - 1024)))
-    lines = jnp.concatenate([line(array) for array in singles] + [gains], axis=0)
     positions = lax.axis_index("seq") * SECTION + jnp.arange(SECTION, dtype=jnp.int32)
     cosine, sine = rotation(positions)
-    turn = jnp.concatenate([cosine, cosine, -sine, sine], axis=1)
     return encode(
-        patch_counts, image_offsets, patches[0], lines, turn, vision_qkv, vision_proj, merge_weight, text_embed,
-        qkv_weight,
+        patch_counts, image_offsets, patches[0], vision_gain, vision_shift, vision_proj_bias, merge_gain, merge_shift,
+        vision_qkv_bias, merge_bias, norm_gain, qkv_bias, cosine, sine, vision_qkv.T, vision_proj, merge_weight,
+        text_embed, qkv_weight,
     )
 
 

time: 171 us -> 161 us (0.942)
  local copies, waits for them, and re-layouts: 10.4 us -> 1.87 us
    broadcast_in_dim x8 -> x0, local copies, waits for them, and re-layouts: 3.53 us -> none  [line(): return jnp.pad(array.astype(f32), (0, VW - array.shape[0]))[None]]
    sin x0 -> x1, other arithmetic: none -> 1.81 us  [rotation(): return (jnp.cos(angles), jnp.sin(angles))]
where the time goes in v6:
time: 161 us; the launch traced here: 158 us
  Pallas kernels  153 us (95%)
  local copies, waits for them, and re-layouts  1.87 us (1%)
  other arithmetic  1.83 us (1%)
    pallas_call x1, Pallas kernels, encode(): pl.pallas_call(vision_kernel, out_shape=jax.ShapeDtypeStruct((HALF, 2 * O...  153 us

profile of v6, /device:TPU:102, one launch (start us, length us, event | category | flops | bytes accessed | tf_op | source)
XLA Modules:
  0.0 158.3 jit_solution(2730229392025454619)
XLA Ops:
  1.3 1.8 %multiply_sine_fusion = (f32[512,64]{1,0:T(8,128)}, f32[512,64]{1,0:T(8,128)}) fusion(f32[64]{0:T(128)S(1)} %multiply_power_fusion, f32[512]{0:T(512)S(1)} %add_convert_fusion), kind=kLoop, calls=%fused_computation | loop fusion | flops 32768 | bytes 264448 | tf_op jit(solution)/shard_map/sin | solution.py:30
  3.1 153.3 %shard_map.163 = bf16[256,1024]{1,0:T(8,128)(2,1)} custom-call(s32[1]{0:T(128)S(6)} %copy.19.count_ref, s32[1]{0:T(128)S(6)} %copy.20.start_ref, bf16[1024,1280]{1,0:T(8,128)(2,1)} %bitcast.2, f32[1280]{0:T(1024)} %gain_ref.1, f32[1280]{0:T(1024)} %shift_ref.1, f32[1280]{0:T(1024)} %proj_bias_ref.1, f32[1280]{0:T(1024)} %merge_gain_ref.1, ...), custom_call_target="tpu_custom_call" | custom-call | tf_op jit(solution)/shard_map/pallas_call | solution.py:643
  156.4 1.9 %copy.21 = bf16[256,1024]{1,0:T(8,128)(2,1)} copy(bf16[256,1024]{1,0:T(8,128)(2,1)} %shard_map.163) | data formatting | bytes 1048576
  (2 shorter events, 0.0 us)

commit v7 on v6

--- a/solution.py
+++ b/solution.py
@@ -486,8 +486,8 @@
     part_out[:, : 4 * HEAD] = taken(1 - img, 4 * HEAD, 0).astype(jnp.bfloat16)
     part_out[:, 4 * HEAD :] = taken(1 - img, HEAD, 8 * HEAD).astype(jnp.bfloat16)
     sums[0] = jnp.sum(squares[...].T, axis=0, keepdims=True) + jnp.zeros((8, SECTION), jnp.float32)
-    for c in trade:
-        c.start()
+    trade[0].start()
+    trade[1].start()
     gather_one = grid_gather(
         copy, 90,
         lambda a, b: buf.at[img, a, b],
@@ -520,13 +520,6 @@
     swap = copy(buf.at[img, x, z], buf.at[img, x, z], 88, other)
     swap.start()
     gather_one[0]()
-    trade[2].wait()
-    heads = [settle(taken(img, 4 * HEAD, 0)[:, n * HEAD : n * HEAD + HEAD], n)[1].astype(jnp.bfloat16) for n in range(4)]
-    for n in range(2):
-        lent[:, n * HEAD : n * HEAD + HEAD] = heads[2 + n]
-        query[pl.ds(n * SECTION, SECTION), :] = heads[n]
-    lend = copy(lent, guest, 89, {"seq": mirror})
-    lend.start()
     rows_all = 2 * SECTION
     ones = jnp.ones((SECTION, HEAD), jnp.bfloat16)
     tiles = SECTION // HEAD
@@ -586,24 +579,32 @@
 
     swap.wait()
     gather_two[0]()
-    block(0, seq, True)
+    trade[2].start()
     gather_one[1]()
     gather_two[1]()
     gather_one[2]()
     gather_two[2]()
+    trade[2].wait()
+    heads = [settle(taken(img, 4 * HEAD, 0)[:, n * HEAD : n * HEAD + HEAD], n)[1].astype(jnp.bfloat16) for n in range(4)]
+    for n in range(2):
+        lent[:, n * HEAD : n * HEAD + HEAD] = heads[2 + n]
+        query[pl.ds(n * SECTION, SECTION), :] = heads[n]
+    lend = copy(lent, guest, 89, {"seq": mirror})
+    lend.start()
+    block(0, seq, True)
+    gather_one[3]()
+    gather_two[3]()
+    gather_one[4]()
+    gather_two[4]()
     lend.wait()
     for head in range(2):
         query[pl.ds(rows_all + head * SECTION, SECTION), :] = guest[:, head * HEAD : (head + 1) * HEAD]
     visit(1, 0, 0)
     both(2, lambda n: (1 + 2 * n, 0))
-    gather_one[3]()
-    gather_two[3]()
-    both(2, lambda n: (0, 1 + 2 * n))
-    gather_one[4]()
-    gather_two[4]()
-    block(1, mirror, True)
     gather_one[5]()
     gather_two[5]()
+    block(1, mirror, True)
+    both(2, lambda n: (0, 1 + 2 * n))
     both(4, lambda n: (1 + 2 * (n // 2), 1 + 2 * (n % 2)))
     gather_one[6]()
     gather_two[6]()

time: 161 us -> 158 us (0.981)
  Pallas kernels: 153 us -> 151 us
    pallas_call x1, Pallas kernels: 153 us -> 151 us  [encode(): pl.pallas_call(vision_kernel, out_shape=jax.ShapeDtypeStruct((HALF, 2 * O...]
where the time goes in v7:
time: 158 us; the launch traced here: 156 us
  Pallas kernels  151 us (96%)
  local copies, waits for them, and re-layouts  1.87 us (1%)
  other arithmetic  1.83 us (1%)
    pallas_call x1, Pallas kernels, encode(): pl.pallas_call(vision_kernel, out_shape=jax.ShapeDtypeStruct((HALF, 2 * O...  151 us

profile of v7, /device:TPU:102, one launch (start us, length us, event | category | flops | bytes accessed | tf_op | source)
XLA Modules:
  0.0 155.9 jit_solution(1647598506221071429)
XLA Ops:
  1.3 1.8 %multiply_sine_fusion = (f32[512,64]{1,0:T(8,128)}, f32[512,64]{1,0:T(8,128)}) fusion(f32[64]{0:T(128)S(1)} %multiply_power_fusion, f32[512]{0:T(512)S(1)} %add_convert_fusion), kind=kLoop, calls=%fused_computation | loop fusion | flops 32768 | bytes 264448 | tf_op jit(solution)/shard_map/sin | solution.py:30
  3.1 150.9 %shard_map.163 = bf16[256,1024]{1,0:T(8,128)(2,1)} custom-call(s32[1]{0:T(128)S(6)} %copy.19.count_ref, s32[1]{0:T(128)S(6)} %copy.20.start_ref, bf16[1024,1280]{1,0:T(8,128)(2,1)} %bitcast.2, f32[1280]{0:T(1024)} %gain_ref.1, f32[1280]{0:T(1024)} %shift_ref.1, f32[1280]{0:T(1024)} %proj_bias_ref.1, f32[1280]{0:T(1024)} %merge_gain_ref.1, ...), custom_call_target="tpu_custom_call" | custom-call | tf_op jit(solution)/shard_map/pallas_call | solution.py:644
  154.1 1.9 %copy.21 = bf16[256,1024]{1,0:T(8,128)(2,1)} copy(bf16[256,1024]{1,0:T(8,128)(2,1)} %shard_map.163) | data formatting | bytes 1048576
  (2 shorter events, 0.0 us)

commit v8 on v7

--- a/solution.py
+++ b/solution.py
@@ -196,8 +196,7 @@
         rows_ref[n : n + 1, : ref.shape[0]] = ref[...].astype(jnp.float32)[None, :]
     bias_row = bias_ref[...].astype(jnp.float32)[None, :]
     q_bias = jnp.where(img == 0, bias_row[:, : 4 * HEAD], bias_row[:, 4 * HEAD : 8 * HEAD])
-    kv_bias = jnp.where(img == 0, bias_row[:, 8 * HEAD : 9 * HEAD], bias_row[:, 9 * HEAD :])
-    rows_ref[7:8, : 5 * HEAD] = jnp.concatenate([q_bias, kv_bias], axis=1)
+    rows_ref[7:8, : 6 * HEAD] = jnp.concatenate([q_bias, bias_row[:, 8 * HEAD :]], axis=1)
     norm_row = norm_ref[...].astype(jnp.float32)[None, :]
     for n in range(8):
         rows_ref[8 + n : 9 + n, :1024] = norm_row[:, n * 1024 : (n + 1) * 1024]
@@ -278,7 +277,7 @@
         for n in range(2)
     ]
     other = {"img": 1 - img}
-    quarter, fifth = pl.ds(0, 4 * HEAD), pl.ds(4 * HEAD, HEAD)
+    quarter, fifth = pl.ds(0, 4 * HEAD), pl.ds(4 * HEAD, 2 * HEAD)
     trade = [
         copy(sums.at[0], sums.at[1], 47, other),
         copy(part_out.at[:, fifth], part_in.at[:, fifth], 46, other),
@@ -484,7 +483,7 @@
         return total[:, pl.ds(pl.multiple_of(start + side * size, HEAD), size)]
 
     part_out[:, : 4 * HEAD] = taken(1 - img, 4 * HEAD, 0).astype(jnp.bfloat16)
-    part_out[:, 4 * HEAD :] = taken(1 - img, HEAD, 8 * HEAD).astype(jnp.bfloat16)
+    part_out[:, 4 * HEAD :] = total[:, 8 * HEAD :].astype(jnp.bfloat16)
     sums[0] = jnp.sum(squares[...].T, axis=0, keepdims=True) + jnp.zeros((8, SECTION), jnp.float32)
     trade[0].start()
     trade[1].start()
@@ -514,11 +513,10 @@
         return head, head * cosine + pltpu.roll(head, HEAD // 2, 1) * sine
 
     trade[1].wait()
-    plain, turned = settle(taken(img, HEAD, 8 * HEAD), OWN_HEADS)
+    turned = settle(total[:, 8 * HEAD : 9 * HEAD], OWN_HEADS)[1]
     columns = [turned[n * HEAD : (n + 1) * HEAD].T for n in range(SECTION // HEAD)]
-    buf[img, x, z] = jnp.where(img == 0, jnp.concatenate(columns, axis=0), plain).astype(jnp.bfloat16)
-    swap = copy(buf.at[img, x, z], buf.at[img, x, z], 88, other)
-    swap.start()
+    buf[0, x, z] = jnp.concatenate(columns, axis=0).astype(jnp.bfloat16)
+    buf[1, x, z] = settle(total[:, 9 * HEAD :], OWN_HEADS + 1)[0].astype(jnp.bfloat16)
     gather_one[0]()
     rows_all = 2 * SECTION
     ones = jnp.ones((SECTION, HEAD), jnp.bfloat16)
@@ -577,7 +575,6 @@
             parts.append((total[:, :HEAD] / total[:, HEAD:]).astype(jnp.bfloat16))
         return jnp.concatenate(parts, axis=1)
 
-    swap.wait()
     gather_two[0]()
     trade[2].start()
     gather_one[1]()
@@ -665,8 +662,8 @@
             pltpu.VMEM((SECTION, 10 * HEAD), f32),
             pltpu.VMEM((SECTION, HEAD), f32),
             pltpu.VMEM((2, 8, SECTION), f32),
-            pltpu.VMEM((SECTION, 5 * HEAD), bf16),
-            pltpu.VMEM((SECTION, 5 * HEAD), bf16),
+            pltpu.VMEM((SECTION, 6 * HEAD), bf16),
+            pltpu.VMEM((SECTION, 6 * HEAD), bf16),
             pltpu.VMEM((2, 4, 4, SECTION, HEAD), bf16),
             pltpu.VMEM((SECTION, 2 * HEAD), bf16),
             pltpu.VMEM((4 * SECTION, HEAD), f32),

time: 158 us -> 158 us (level)
  no operation moved by 1% of the time
where the time goes in v8:
time: 158 us; the launch traced here: 155 us
  Pallas kernels  150 us (95%)
  local copies, waits for them, and re-layouts  1.87 us (1%)
  other arithmetic  1.83 us (1%)
    pallas_call x1, Pallas kernels, encode(): pl.pallas_call(vision_kernel, out_shape=jax.ShapeDtypeStruct((HALF, 2 * O...  150 us

profile of v8, /device:TPU:102, one launch (start us, length us, event | category | flops | bytes accessed | tf_op | source)
XLA Modules:
  0.0 154.8 jit_solution(2941231064918837614)
XLA Ops:
  1.3 1.8 %multiply_sine_fusion = (f32[512,64]{1,0:T(8,128)}, f32[512,64]{1,0:T(8,128)}) fusion(f32[64]{0:T(128)S(1)} %multiply_power_fusion, f32[512]{0:T(512)S(1)} %add_convert_fusion), kind=kLoop, calls=%fused_computation | loop fusion | flops 32768 | bytes 264448 | tf_op jit(solution)/shard_map/sin | solution.py:30
  3.1 149.8 %shard_map.163 = bf16[256,1024]{1,0:T(8,128)(2,1)} custom-call(s32[1]{0:T(128)S(6)} %copy.19.count_ref, s32[1]{0:T(128)S(6)} %copy.20.start_ref, bf16[1024,1280]{1,0:T(8,128)(2,1)} %bitcast.2, f32[1280]{0:T(1024)} %gain_ref.1, f32[1280]{0:T(1024)} %shift_ref.1, f32[1280]{0:T(1024)} %proj_bias_ref.1, f32[1280]{0:T(1024)} %merge_gain_ref.1, ...), custom_call_target="tpu_custom_call" | custom-call | tf_op jit(solution)/shard_map/pallas_call | solution.py:641
  153.0 1.9 %copy.21 = bf16[256,1024]{1,0:T(8,128)(2,1)} copy(bf16[256,1024]{1,0:T(8,128)(2,1)} %shard_map.163) | data formatting | bytes 1048576
  (2 shorter events, 0.0 us)
